TPU v7x, 128 devices: a whole 4x4x4 slice. The times are simulated.
128 devices in a mesh: seq: 8 (over y, x_hi), vocab: 16 (over z, x_lo, core).
Axes of the slice: x: 4 (x_hi: 2, x_lo: 2; x = x_hi * 2 + x_lo), y: 4, z: 4, core: 2. Of those that a mesh axis runs over, the one named last changes fastest.
Arguments:
- hidden: bfloat16 [1024, 7168], P('seq', 'vocab'), may hold values from -150 to 150
- next_ids: int32 [1024], P('seq'), may hold values from 0 to 65535
- targets: int32 [1024], P('seq'), may hold values from 0 to 65535
- embed_table: bfloat16 [65536, 7168], P('seq', 'vocab'), may hold values from -80 to 80
- gain_hidden: float32 [7168], P('vocab'), may hold values from 0.5 to 1.5
- gain_embed: float32 [7168], P('vocab'), may hold values from 0.5 to 1.5
- proj_hidden: bfloat16 [7168, 7168], P('vocab', 'seq'), may hold values from -0.0625 to 0.0625
- proj_embed: bfloat16 [7168, 7168], P('vocab', 'seq'), may hold values from -0.0625 to 0.0625
- gain_final: float32 [7168], P('seq'), may hold values from 0.5 to 1.5
- head_weight: bfloat16 [65536, 7168], P(('seq', 'vocab')), may hold values from -3.30718914 to 3.30718914
Outputs:
- loss_mean: float32 [], replicated
- head_grad: bfloat16 [65536, 7168], P(('seq', 'vocab'))
All inputs are finite; a program needn't handle non-finite values.
Results may differ from a plain program's by a relative error of at most 0.011.
Values may be sent and summed in bfloat16 or wider, within the bound.
A program may use at most 128 MiB of HBM per device.

v0:
```python
import jax
import jax.numpy as jnp
from jax import lax
from jax.sharding import PartitionSpec as P

D = 7168


EPSILON = 1e-06


def body(
    hidden,
    next_ids,
    targets,
    embed_table,
    gain_hidden,
    gain_embed,
    proj_hidden,
    proj_embed,
    gain_final,
    head_weight,
):
    seq_pos = lax.axis_index("seq")
    vocab_pos = lax.axis_index("vocab")
    vocab_count = lax.axis_size("vocab")
    all_ids, all_targets = (
        lax.all_gather(next_ids, "seq", axis=0, tiled=True),
        lax.all_gather(targets, "seq", axis=0, tiled=True),
    )
    table_rows = embed_table.shape[0]
    local_ids = all_ids - seq_pos * table_rows
    inside = (local_ids >= 0) & (local_ids < table_rows)
    looked_up = jnp.take(embed_table, jnp.clip(local_ids, 0, table_rows - 1), axis=0)
    looked_up = jnp.where(inside[:, None], looked_up, jnp.zeros((), jnp.bfloat16))
    embedded = lax.psum(looked_up, "seq").astype(jnp.float32)
    all_hidden = lax.all_gather(hidden, "seq", axis=0, tiled=True).astype(jnp.float32)
    hidden_sq, embed_sq = lax.psum(
        (jnp.sum(all_hidden * all_hidden, axis=1), jnp.sum(embedded * embedded, axis=1)), "vocab"
    )
    normed_hidden = (all_hidden * lax.rsqrt(hidden_sq / D + EPSILON)[:, None] * gain_hidden).astype(
        jnp.bfloat16
    )
    normed_embed = (embedded * lax.rsqrt(embed_sq / D + EPSILON)[:, None] * gain_embed).astype(
        jnp.bfloat16
    )
    projected = lax.psum_scatter(
        jnp.dot(normed_hidden, proj_hidden, preferred_element_type=jnp.float32)
        + jnp.dot(normed_embed, proj_embed, preferred_element_type=jnp.float32),
        "vocab",
        scatter_dimension=0,
        tiled=True,
    )
    proj_sq = lax.psum(jnp.sum(projected * projected, axis=1), "seq")
    final_rows = (projected * lax.rsqrt(proj_sq / D + EPSILON)[:, None] * gain_final).astype(
        jnp.bfloat16
    )
    vocab_rows = head_weight.shape[0]
    wide_rows = lax.all_gather(final_rows, "seq", axis=1, tiled=True)
    block_rows = lax.all_gather(wide_rows, "vocab", axis=0, tiled=True)
    scores = lax.dot_general(
        block_rows, head_weight, (((1,), (1,)), ((), ())), preferred_element_type=jnp.float32
    )
    first_entry = (seq_pos * vocab_count + vocab_pos) * vocab_rows
    columns = first_entry + lax.broadcasted_iota(jnp.int32, scores.shape, 1)
    matches = columns == all_targets[:, None]
    local_peak = jnp.max(scores, axis=1)
    local_chosen = jnp.sum(jnp.where(matches, scores, 0.0), axis=1)
    row_peak = lax.pmax(local_peak, ("seq", "vocab"))
    totals, chosen = lax.psum(
        (jnp.sum(jnp.exp(scores - row_peak[:, None]), axis=1), local_chosen), ("seq", "vocab")
    )
    log_total = row_peak + jnp.log(totals)
    loss_mean = jnp.mean(log_total - chosen)
    logit_grad = (jnp.exp(scores - log_total[:, None]) - matches.astype(jnp.float32)).astype(
        jnp.bfloat16
    )
    head_grad = lax.dot_general(
        logit_grad, block_rows, (((0,), (0,)), ((), ())), preferred_element_type=jnp.float32
    ).astype(jnp.bfloat16)
    return (loss_mean, head_grad)


def solution(mesh):
    in_specs = (
        P("seq", "vocab"),
        P("seq"),
        P("seq"),
        P("seq", "vocab"),
        P("vocab"),
        P("vocab"),
        P("vocab", "seq"),
        P("vocab", "seq"),
        P("seq"),
        P(("seq", "vocab"), None),
    )
    out_specs = (P(), P(("seq", "vocab"), None))
    return jax.shard_map(body, mesh=mesh, in_specs=in_specs, out_specs=out_specs, check_vma=False)
```

profile of v0, /device:TPU:1, one launch (start us, length us, event | category | flops | bytes accessed | tf_op | source)
XLA Modules:
  0.0 553.4 jit_solution(2484946210938634185)
XLA Ops:
  7.2 0.0 copy-start
  7.2 0.0 all-reduce.4.cloned.1.call-start
  7.2 20.8 %all-gather = s32[8,1,128]{2,1,0:T(1,128)S(1)} all-gather(s32[1,1,128]{2,1,0:T(1,128)} %bitcast.22), channel_id=1, replica_groups=mesh['seq'=8,'vocab'=16] {'seq'}, dimensions={0}, use_global_device_ids=true | all-gather | bytes 4608 | tf_op jit(solution)/shard_map/all_gather | solution.py:28
  28.1 11.6 %copy.15 = bf16[8192,448]{1,0:T(8,128)(2,1)} copy(bf16[8192,448]{0,1:T(8,128)(2,1)} %param.13) | data formatting | bytes 14680064 | tf_op args[3]
  39.7 8.4 %gather_fusion = bf16[1024,448]{1,0:T(8,128)(2,1)S(1)} fusion(bf16[8192,448]{1,0:T(8,128)(2,1)} %copy.15, s32[1024]{0:T(1024)S(1)} %fusion.20), kind=kCustom, calls=%fused_computation | custom fusion | bytes 1839104 | tf_op jit(solution)/shard_map/jit(_take)/gather | solution.py:34
  48.1 0.0 copy-start.3
  48.2 1.6 select_select_fusion
  49.8 0.0 copy-start.7
  49.8 0.0 all-reduce.4.cloned.1.call-update
  49.8 0.0 reduce-scatter.2.cloned.1.call-start
  49.8 0.0 copy-done.3
  49.8 35.0 %all_gather.15 = bf16[1024,448]{0,1:T(8,128)(2,1)S(1)} all-gather(bf16[128,448]{0,1:T(8,128)(2,1)S(1)} %copy-done.3), channel_id=1, replica_groups=mesh['seq'=8,'vocab'=16] {'seq'}, dimensions={0}, use_global_device_ids=true | all-gather | bytes 1032192 | tf_op jit(solution)/shard_map/all_gather | solution.py:37
  84.9 0.2 fusion.6
  85.1 56.9 %all-reduce.4.cloned.1.call-done = bf16[1024,448]{1,0:T(8,128)(2,1)} async-done(((bf16[1024,448]{1,0:T(8,128)(2,1)}), bf16[1024,448]{1,0:T(8,128)(2,1)}) %all-reduce.4.cloned.1.call-update) | async-done | bytes 917520 | tf_op jit(solution)/shard_map/psum | solution.py:36
  142.0 1.5 fusion
  143.5 32.9 %all-reduce.1 = (f32[1024]{0:T(1024)S(1)}, f32[1024]{0:T(1024)S(1)}) all-reduce(f32[1024]{0:T(1024)S(1)} %fusion.6, f32[1024]{0:T(1024)S(1)} %fusion), channel_id=1, replica_groups=mesh['seq'=8,'vocab'=16] {'vocab'}, use_global_device_ids=true, to_apply=%region_1.2 | all-reduce | flops 2048 | bytes 16384 | tf_op jit(solution)/shard_map/psum | solution.py:38
  176.4 0.0 copy-done
  176.4 0.0 copy-done.7
  176.4 0.0 copy-start.1
  176.4 0.0 copy-start.2
  176.5 0.0 copy-start.5
  176.5 1.4 fusion.16
  177.9 0.0 copy-done.1
  177.9 0.0 copy-done.2
  177.9 0.0 copy-done.5
  177.9 3.1 convolution_add_fusion
  181.0 0.0 copy-start.4
  181.1 0.0 reduce-scatter.2.cloned.1.call-update
  181.1 0.0 copy-start.6
  181.1 0.0 all-gather.4.cloned.1.call-start
  181.1 61.0 %reduce-scatter.2.cloned.1.call-done = f32[64,896]{1,0:T(8,128)} async-done(((f32[1024,896]{1,0:T(8,128)}), f32[64,896]{1,0:T(8,128)}) %reduce-scatter.2.cloned.1.call-update) | async-done | bytes 229392 | tf_op jit(solution)/shard_map/reduce_scatter | solution.py:47
  242.1 1.1 multiply_reduce_fusion
  243.2 20.2 %psum.45 = f32[64]{0:T(128)S(1)} all-reduce(f32[64]{0:T(128)S(1)} %multiply_reduce_fusion), channel_id=1, replica_groups=mesh['seq'=8,'vocab'=16] {'seq'}, use_global_device_ids=true, to_apply=%region_7.8 | all-reduce | flops 64 | bytes 512 | tf_op jit(solution)/shard_map/psum | solution.py:54
  263.4 0.0 copy-done.4
  263.4 1.0 multiply_convert_fusion
  264.4 35.3 %all_gather.17 = bf16[64,7168]{1,0:T(8,128)(2,1)} all-gather(bf16[64,896]{1,0:T(8,128)(2,1)S(1)} %multiply_convert_fusion), channel_id=1, replica_groups=mesh['seq'=8,'vocab'=16] {'seq'}, dimensions={1}, use_global_device_ids=true | all-gather | bytes 1032192 | tf_op jit(solution)/shard_map/all_gather | solution.py:59
  299.7 0.0 all-gather.4.cloned.1.call-update
  299.7 0.0 copy-done.6
  299.7 14.7 %all-gather.1 = s32[8,1,128]{2,1,0:T(1,128)S(1)} all-gather(s32[1,1,128]{2,1,0:T(1,128)S(1)} %bitcast.23), channel_id=1, replica_groups=mesh['seq'=8,'vocab'=16] {'seq'}, dimensions={0}, use_global_device_ids=true | all-gather | bytes 4608 | tf_op jit(solution)/shard_map/all_gather | solution.py:29
  314.5 72.1 %all-gather.4.cloned.1.call-done = bf16[1024,7168]{1,0:T(8,128)(2,1)} async-done(((bf16[64,7168]{1,0:T(8,128)(2,1)}), bf16[1024,7168]{1,0:T(8,128)(2,1)}) %all-gather.4.cloned.1.call-update) | async-done | bytes 14680080 | tf_op jit(solution)/shard_map/all_gather | solution.py:60
  386.6 13.2 %fusion.21 = (f32[1024]{0:T(1024)S(1)}, f32[1024,512]{0,1:T(8,128)S(1)}) fusion(bf16[1024,7168]{1,0:T(8,128)(2,1)} %all-gather.4.cloned.1.call-done, bf16[512,7168]{1,0:T(8,128)(2,1)} %param.19), kind=kOutput, calls=%fused_computation.40 | convolution fusion | flops 7516716032 | bytes 24121344 | tf_op jit(solution)/shard_map/dot_general | solution.py:61
  399.8 65.7 %pmax.7 = f32[1024]{0:T(1024)S(1)} all-reduce(f32[1024]{0:T(1024)S(1)} %get-tuple-element.10), channel_id=1, replica_groups=mesh['seq'=8,'vocab'=16] {'seq','vocab'}, use_global_device_ids=true, to_apply=%region_9.10 | all-reduce | flops 1024 | bytes 8192 | tf_op jit(solution)/shard_map/pmax | solution.py:69
  465.5 0.5 fusion.3
  466.0 63.2 %all-reduce = (f32[1024]{0:T(1024)S(1)}, f32[1024]{0:T(1024)S(1)}) all-reduce(f32[1024]{0:T(1024)S(1)} %get-tuple-element.3, f32[1024]{0:T(1024)S(1)} %get-tuple-element.2), channel_id=1, replica_groups=mesh['seq'=8,'vocab'=16] {'seq','vocab'}, use_global_device_ids=true, to_apply=%region_11.12 | all-reduce | flops 2048 | bytes 16384 | tf_op jit(solution)/shard_map/psum | solution.py:70
  529.1 0.6 subtract_reduce_fusion
  530.4 15.3 %convolution_convert_fusion = bf16[512,7168]{1,0:T(8,128)(2,1)} fusion(bf16[1024,7168]{1,0:T(8,128)(2,1)} %all-gather.4.cloned.1.call-done, f32[1024,512]{0,1:T(8,128)S(1)} %get-tuple-element.11, f32[1024]{0:T(1024)S(1)} %get-tuple-element.9, s32[1024]{0:T(1024)S(1)} %bitcast.21, s32[512]{0:T(512)S(1)} %iota_add_fusion), kind=kOutput, calls=%fused_computation.1 | convolution fusion | flops 7522484224 | bytes 24127488 | tf_op jit(solution)/shard_map/dot_general | solution.py:78
  (6 shorter events, 0.0 us)
Async XLA Ops:
  7.2 169.3 %copy-start = (bf16[448,896]{1,0:T(8,128)(2,1)S(1)}, bf16[448,896]{1,0:T(8,128)(2,1)}, u32[]{:S(2)}) copy-start(bf16[448,896]{1,0:T(8,128)(2,1)} %param.16) | copy-start | bytes 2408452
  7.2 134.8 %all-reduce.4.cloned.1.call-start = ((), (), s32[]{:S(2)}) async-start(), calls=%async_computation.1 | async-start | bytes 2097152 | tf_op jit(solution)/shard_map/psum | solution.py:36
  48.1 1.7 copy-start.3
  49.8 126.7 %copy-start.7 = (f32[448]{0:T(512)S(1)}, f32[448]{0:T(512)}, u32[]{:S(2)}) copy-start(f32[448]{0:T(512)} %param.14) | copy-start | bytes 5380
  49.8 192.3 %reduce-scatter.2.cloned.1.call-start = ((), (), s32[]{:S(2)}) async-start(), calls=%async_computation.2 | async-start | bytes 3899392 | tf_op jit(solution)/shard_map/reduce_scatter | solution.py:47
  176.4 1.4 copy-start.1
  176.4 1.4 copy-start.2
  176.5 1.4 copy-start.5
  181.0 82.3 %copy-start.4 = (f32[896]{0:T(1024)S(1)}, f32[896]{0:T(1024)}, u32[]{:S(2)}) copy-start(f32[896]{0:T(1024)} %param.18) | copy-start | bytes 10756
  181.1 118.7 %copy-start.6 = (s32[128]{0:T(128)S(1)}, s32[128]{0:T(128)}, u32[]{:S(2)}) copy-start(s32[128]{0:T(128)} %param.12) | copy-start | bytes 1540
  181.1 205.6 %all-gather.4.cloned.1.call-start = ((), (), s32[]{:S(2)}) async-start(), calls=%async_computation.3 | async-start | bytes 15597568 | tf_op jit(solution)/shard_map/all_gather | solution.py:60
Sparse Core Ops, SparseCore 0:
  49.9 92.0 all-reduce.3
  181.2 60.8 reduce-scatter.1
  299.8 86.7 all-gather.3
where the time goes:
time: 554 us; the launch traced here: 553 us
  blocking collectives  288 us (52%)
  waiting for transfers between devices  190 us (34%)
  matrix products  33 us (6%)
  local copies, waits for them, and re-layouts  20.1 us (4%)
  between operations  15.7 us (3%)
  other arithmetic  6.57 us (1%)
    all_gather x1, waiting for transfers between devices, body(): block_rows = lax.all_gather(wide_rows, 'vocab', axis=0, tiled=True)  72.1 us
    pmax x1, blocking collectives, body(): row_peak = lax.pmax(local_peak, ('seq', 'vocab'))  65.7 us
    psum x1, blocking collectives, body(): lax.psum((jnp.sum(jnp.exp(scores - row_peak[:, None]), axis=1), local_cho...  63.2 us
    reduce_scatter x1, waiting for transfers between devices, body(): lax.psum_scatter(jnp.dot(normed_hidden, proj_hidden, preferred_element_ty...  61 us
    psum x1, waiting for transfers between devices, body(): embedded = lax.psum(looked_up, 'seq').astype(jnp.float32)  56.9 us
    all_gather x1, blocking collectives, body(): wide_rows = lax.all_gather(final_rows, 'seq', axis=1, tiled=True)  35.3 us
    all_gather x1, blocking collectives, body(): lax.all_gather(hidden, 'seq', axis=0, tiled=True).astype(jnp.float32)  35 us
    psum x1, blocking collectives, body(): lax.psum((jnp.sum(all_hidden * all_hidden, axis=1), jnp.sum(embedded * em...  32.9 us
  transfers between devices with their start and end apart: 3, of which 3 were waited for; matrix products, arithmetic and copies ran while one was open for 0% of the time, Pallas kernels for 0%

commit v1 on v0

v1 whole, which is shorter than its diff:
```python
import jax
import jax.numpy as jnp
from jax import lax
from jax.experimental import pallas as pl
from jax.experimental.pallas import tpu as pltpu
from jax.sharding import PartitionSpec as P

MESH = pl.DeviceIdType.MESH
D = 7168
EPSILON = 1e-06
HIGH, LOW = 48, 16
ORDERS = (((2, 0, 1), (0, 1, 2)), ((2, 1, 0), (1, 0, 2)))
ROWS = ((0, HIGH), (HIGH, LOW))


def coordinates():
    seq, vocab = lax.axis_index("seq"), lax.axis_index("vocab")
    return (
        (2 * lax.rem(seq, 2) + lax.rem(lax.div(vocab, 2), 2), lax.div(seq, 2), lax.div(vocab, 4)),
        lax.rem(vocab, 2),
    )


def device(pos, core):
    x, y, z = pos
    return (2 * y + lax.div(x, 2), 4 * z + 2 * lax.rem(x, 2) + core)


def shifted(pos, axis, by):
    moved = list(pos)
    moved[axis] = lax.rem(pos[axis] + (by + 4), 4)
    return tuple(moved)


def greet(peers):
    barrier = pltpu.get_barrier_semaphore()
    for peer in peers:
        pl.semaphore_signal(barrier, inc=1, device_id=peer, device_id_type=MESH)
    pl.semaphore_wait(barrier, len(peers))


def head_kernel(
    block_ref, head_ref, target_ref, grad_ref, loss_ref, rows_out,
    rows, head, scores, stats, vstats, sstats,
    ring_send, ring_recv, pair_send, pair_recv, stat_send, stat_recv, local_sem, out_sem,
):
    pos, core = coordinates()
    seq, vocab = lax.axis_index("seq"), lax.axis_index("vocab")
    x, y, z = pos
    head_copies = [
        pltpu.make_async_copy(
            head_ref.at[:, pl.ds(896 * i, 896)], head.at[i], local_sem.at[i]
        )
        for i in range(8)
    ]
    for copy in head_copies:
        copy.start()
    vocab_peers = [(seq, lax.rem(vocab + i, 16)) for i in range(1, 16)]
    seq_peers = [(lax.rem(seq + i, 8), vocab) for i in range(1, 8)]
    across = device(shifted(pos, 0, 1 - 2 * (1 - lax.rem(x, 2))), core)
    greet(vocab_peers + seq_peers + [across])

    rows[x, y, z, core] = block_ref[...]

    def unit(part, at, axis, half=None):
        index = list(at)
        if axis is not None:
            index[axis] = pl.ds(0, 4) if half is None else pl.ds(2 * half, 2)
        return index, ROWS[part]

    def ref_of(where, which):
        index, (first, count) = where
        return rows.at[index[0], index[1], index[2], which, pl.ds(first, count), :]

    def ring(mine, part, number, where, to):
        target = device(to, mine)
        piece = ref_of(where, mine)
        return pltpu.make_async_remote_copy(
            src_ref=piece, dst_ref=piece,
            send_sem=ring_send.at[part, number], recv_sem=ring_recv.at[part, number],
            device_id=target, device_id_type=MESH,
        )

    def pair(part, number, where, which, mine):
        piece = ref_of(where, which)
        return pltpu.make_async_remote_copy(
            src_ref=piece, dst_ref=piece,
            send_sem=pair_send.at[part, number], recv_sem=pair_recv.at[part, number],
            device_id=device(pos, 1 - mine), device_id_type=MESH,
        )

    def line_units(order, part):
        a, b, c = order
        lines = [(1, pos)]
        lines += [(2, shifted(pos, b, -1)), (2, shifted(pos, b, 1)), (3, shifted(pos, b, 2))]
        middles = [lines[i][1] for i in range(4)]
        for j, middle in enumerate(middles):
            lines += [(4 + j, shifted(middle, c, -1)), (4 + j, shifted(middle, c, 1))]
        for j, middle in enumerate(middles):
            lines.append((8 + j, shifted(middle, c, 2)))
        return [(step, unit(part, at, a)) for step, at in lines]

    def own_step(mine, step):
        for part in range(2):
            a, b, c = ORDERS[mine][part]

            def send(number, where, to):
                ring(mine, part, number, where, to).start()

            def recv(number, where):
                ring(mine, part, number, where, pos).wait_recv()

            def up(axis):
                return shifted(pos, axis, 1)

            def down(axis):
                return shifted(pos, axis, -1)

            middles = [pos, down(b), up(b), shifted(pos, b, 2)]

            def spread(j):
                send(7 + 4 * j, unit(part, middles[j], a), up(c))
                send(8 + 4 * j, unit(part, middles[j], a), down(c))

            if step == 0:
                send(0, unit(part, pos, None), up(a))
                send(1, unit(part, pos, None), down(a))
            elif step == 1:
                recv(0, unit(part, down(a), None))
                send(2, unit(part, down(a), None), up(a))
                recv(1, unit(part, up(a), None))
                recv(2, unit(part, shifted(pos, a, 2), None))
                send(3, unit(part, pos, a), up(b))
                send(4, unit(part, pos, a), down(b))
                spread(0)
            elif step == 2:
                recv(3, unit(part, middles[1], a))
                send(5, unit(part, middles[1], a, 0), up(b))
                recv(4, unit(part, middles[2], a))
                send(6, unit(part, middles[2], a, 1), down(b))
                spread(1)
                spread(2)
            elif step == 3:
                recv(5, unit(part, middles[3], a, 0))
                recv(6, unit(part, middles[3], a, 1))
                spread(3)
            elif step < 8:
                j = step - 4
                before, after = shifted(middles[j], c, -1), shifted(middles[j], c, 1)
                recv(7 + 4 * j, unit(part, before, a))
                send(9 + 4 * j, unit(part, before, a, 0), up(c))
                recv(8 + 4 * j, unit(part, after, a))
                send(10 + 4 * j, unit(part, after, a, 1), down(c))
            else:
                j = step - 8
                far = shifted(middles[j], c, 2)
                recv(9 + 4 * j, unit(part, far, a, 0))
                recv(10 + 4 * j, unit(part, far, a, 1))
            for number, (when, where) in enumerate(line_units(ORDERS[mine][part], part)):
                if when == step:
                    pair(part, number, where, mine, mine).start()

    def pair_step(mine, step):
        for part in range(2):
            for number, (when, where) in enumerate(line_units(ORDERS[1 - mine][part], part)):
                if when == step:
                    pair(part, number, where, 1 - mine, mine).wait_recv()

    def by_core(action, step):
        for mine in range(2):

            @pl.when(core == mine)
            def _():
                action(mine, step)

    x_hi = lax.div(x, 2)

    def multiply(dy, other, part):
        y_at = lax.rem(y + dy + 4, 4)
        hi_at = lax.rem(x_hi + other, 2)
        first, count = ROWS[part]
        taken = rows[pl.ds(2 * hi_at, 2), y_at, :, :, pl.ds(first, count), :].reshape(-1, 896)
        product = lax.dot_general(
            head[2 * y_at + hi_at], taken, (((1,), (1,)), ((), ())), preferred_element_type=jnp.float32
        )
        columns = slice(0, 16 * HIGH) if part == 0 else slice(16 * HIGH, 1024)
        if (dy, other) == (0, 0):
            scores[:, columns] = product
        else:
            scores[:, columns] += product

    out_copies = []

    def write_out(dy, other):
        y_at = lax.rem(y + dy + 4, 4)
        hi_at = lax.rem(x_hi + other, 2)
        piece = (pl.ds(2 * hi_at, 2), y_at)
        copy = pltpu.make_async_copy(rows.at[piece], rows_out.at[piece], out_sem.at[len(out_copies)])
        copy.start()
        out_copies.append(copy)

    ready = {
        4: [(0, 0, 0)],
        6: [(-1, 0, 0), (1, 0, 0)],
        8: [(0, 1, 0)],
        9: [(-1, 1, 0)],
        10: [(2, 0, 0), (1, 1, 0), (0, 0, 1), (-1, 0, 1), (1, 0, 1)],
        11: [(2, 1, 0), (2, 0, 1), (0, 1, 1), (-1, 1, 1), (1, 1, 1), (2, 1, 1)],
    }
    for step in range(13):
        if step < 12:
            by_core(own_step, step)
        if step == 3:
            for copy in head_copies:
                copy.wait()
        if step >= 2:
            by_core(pair_step, step - 1)
            for dy, other, part in ready.get(step - 1, []):
                multiply(dy, other, part)
                if part == 1:
                    write_out(dy, other)

    first_entry = (seq * 16 + vocab) * 512
    entries = first_entry + lax.broadcasted_iota(jnp.int32, (512, 128), 0)
    for q in range(8):
        columns = slice(128 * q, 128 * q + 128)
        part = scores[:, columns]
        peak = jnp.max(part, axis=0, keepdims=True)
        matches = entries == target_ref[q : q + 1, :]
        chosen = jnp.sum(jnp.where(matches, part, 0.0), axis=0, keepdims=True)
        powers = jnp.exp(part - peak)
        scores[:, columns] = powers
        stats[0, q : q + 1, :] = peak
        stats[1, q : q + 1, :] = jnp.sum(powers, axis=0, keepdims=True)
        stats[2, q : q + 1, :] = chosen

    def exchange(slots, me, peers, count, base):
        slots[me] = stats[...]
        copies = []
        for i, peer in enumerate(peers):
            copies.append(pltpu.make_async_remote_copy(
                src_ref=stats, dst_ref=slots.at[me],
                send_sem=stat_send.at[base + i], recv_sem=stat_recv.at[base + i],
                device_id=peer, device_id_type=MESH,
            ))
            copies[-1].start()
        for i in range(len(peers)):
            sender = lax.rem(me - (i + 1) + count, count)
            pltpu.make_async_remote_copy(
                src_ref=stats, dst_ref=slots.at[sender],
                send_sem=stat_send.at[base + i], recv_sem=stat_recv.at[base + i],
                device_id=peers[i], device_id_type=MESH,
            ).wait_recv()
        for copy in copies:
            copy.wait_send()
        peaks = slots[:, 0]
        top = jnp.max(peaks, axis=0)
        total = jnp.sum(slots[:, 1] * jnp.exp(peaks - top[None]), axis=0)
        chosen = jnp.sum(slots[:, 2], axis=0)
        return top, total, chosen

    own_peak = stats[0]
    top, total, chosen = exchange(vstats, vocab, vocab_peers, 16, 0)
    stats[0], stats[1], stats[2] = top, total, chosen
    top, total, chosen = exchange(sstats, seq, seq_peers, 8, 15)
    log_total = top + jnp.log(total)
    loss_ref[0, 0] = jnp.sum(log_total - chosen) / 1024
    stats[0] = jnp.exp(own_peak - log_total)
    for q in range(8):
        columns = slice(128 * q, 128 * q + 128)
        matches = entries == target_ref[q : q + 1, :]
        grad = scores[:, columns] * stats[0, q : q + 1, :] - jnp.where(matches, 1.0, 0.0)
        grad_ref[:, columns] = grad.astype(jnp.bfloat16)

    def finish(mine, _):
        for part in range(2):
            a, b, c = ORDERS[mine][part]
            sizes = [(pos, None, None)] * 3 + [(pos, a, None)] * 2 + [(pos, a, 0)] * 2
            sizes += ([(pos, a, None)] * 2 + [(pos, a, 0)] * 2) * 4
            for number, (at, axis, half) in enumerate(sizes):
                ring(mine, part, number, unit(part, at, axis, half), pos).wait_send()
            for number, (_, where) in enumerate(line_units(ORDERS[mine][part], part)):
                pair(part, number, where, mine, mine).wait_send()

    by_core(finish, 0)
    for copy in out_copies:
        copy.wait()


def head_part(block, head_weight, targets):
    return pl.pallas_call(
        head_kernel,
        out_shape=(
            jax.ShapeDtypeStruct((512, 1024), jnp.bfloat16),
            jax.ShapeDtypeStruct((1, 1), jnp.float32),
            jax.ShapeDtypeStruct((4, 4, 4, 2, 64, 896), jnp.bfloat16),
        ),
        in_specs=[
            pl.BlockSpec(memory_space=pltpu.VMEM),
            pl.BlockSpec(memory_space=pl.ANY),
            pl.BlockSpec(memory_space=pltpu.VMEM),
        ],
        out_specs=(
            pl.BlockSpec(memory_space=pltpu.VMEM),
            pl.BlockSpec(memory_space=pltpu.SMEM),
            pl.BlockSpec(memory_space=pl.ANY),
        ),
        scratch_shapes=[
            pltpu.VMEM((4, 4, 4, 2, 64, 896), jnp.bfloat16),
            pltpu.VMEM((8, 512, 896), jnp.bfloat16),
            pltpu.VMEM((512, 1024), jnp.float32),
            pltpu.VMEM((3, 8, 128), jnp.float32),
            pltpu.VMEM((16, 3, 8, 128), jnp.float32),
            pltpu.VMEM((8, 3, 8, 128), jnp.float32),
            pltpu.SemaphoreType.DMA((2, 23)),
            pltpu.SemaphoreType.DMA((2, 23)),
            pltpu.SemaphoreType.DMA((2, 16)),
            pltpu.SemaphoreType.DMA((2, 16)),
            pltpu.SemaphoreType.DMA((22,)),
            pltpu.SemaphoreType.DMA((22,)),
            pltpu.SemaphoreType.DMA((8,)),
            pltpu.SemaphoreType.DMA((8,)),
        ],
        compiler_params=pltpu.CompilerParams(
            collective_id=2, has_side_effects=True, vmem_limit_bytes=56 * 1024 * 1024
        ),
    )(block, head_weight, targets)


def grad_kernel(grad_ref, rows_ref, out_ref):
    high = rows_ref[:, 0, :, :, 0:HIGH, :].reshape(16 * HIGH, 896)
    low = rows_ref[:, 0, :, :, HIGH:64, :].reshape(16 * LOW, 896)
    out_ref[...] = (
        jnp.dot(grad_ref[:, : 16 * HIGH], high, preferred_element_type=jnp.float32)
        + jnp.dot(grad_ref[:, 16 * HIGH :], low, preferred_element_type=jnp.float32)
    ).astype(jnp.bfloat16)


def head_gradient(grad, rows):
    return pl.pallas_call(
        grad_kernel,
        out_shape=jax.ShapeDtypeStruct((512, D), jnp.bfloat16),
        grid=(8,),
        in_specs=[
            pl.BlockSpec((512, 1024), lambda i: (0, 0)),
            pl.BlockSpec((2, 1, 4, 2, 64, 896), lambda i: (i % 2, i // 2, 0, 0, 0, 0)),
        ],
        out_specs=pl.BlockSpec((512, 896), lambda i: (0, i)),
        compiler_params=pltpu.CompilerParams(vmem_limit_bytes=40 * 1024 * 1024),
    )(grad, rows)


def kernel_order(values):
    split = values.reshape(4, 2, 2, 64).transpose(1, 0, 2, 3)
    parts = [split[..., :HIGH].reshape(-1), split[..., HIGH:].reshape(-1)]
    return jnp.concatenate(parts).reshape(8, 128)


def body(
    hidden,
    next_ids,
    targets,
    embed_table,
    gain_hidden,
    gain_embed,
    proj_hidden,
    proj_embed,
    gain_final,
    head_weight,
):
    seq_pos = lax.axis_index("seq")
    all_ids, all_targets = (
        lax.all_gather(next_ids, "seq", axis=0, tiled=True),
        lax.all_gather(targets, "seq", axis=0, tiled=True),
    )
    table_rows = embed_table.shape[0]
    local_ids = all_ids - seq_pos * table_rows
    inside = (local_ids >= 0) & (local_ids < table_rows)
    looked_up = jnp.take(embed_table, jnp.clip(local_ids, 0, table_rows - 1), axis=0)
    looked_up = jnp.where(inside[:, None], looked_up, jnp.zeros((), jnp.bfloat16))
    embedded = lax.psum(looked_up, "seq").astype(jnp.float32)
    all_hidden = lax.all_gather(hidden, "seq", axis=0, tiled=True).astype(jnp.float32)
    hidden_sq, embed_sq = lax.psum(
        (jnp.sum(all_hidden * all_hidden, axis=1), jnp.sum(embedded * embedded, axis=1)), "vocab"
    )
    normed_hidden = (all_hidden * lax.rsqrt(hidden_sq / D + EPSILON)[:, None] * gain_hidden).astype(
        jnp.bfloat16
    )
    normed_embed = (embedded * lax.rsqrt(embed_sq / D + EPSILON)[:, None] * gain_embed).astype(
        jnp.bfloat16
    )
    projected = lax.psum_scatter(
        jnp.dot(normed_hidden, proj_hidden, preferred_element_type=jnp.float32)
        + jnp.dot(normed_embed, proj_embed, preferred_element_type=jnp.float32),
        "vocab",
        scatter_dimension=0,
        tiled=True,
    )
    proj_sq = lax.psum(jnp.sum(projected * projected, axis=1), "seq")
    final_rows = (projected * lax.rsqrt(proj_sq / D + EPSILON)[:, None] * gain_final).astype(
        jnp.bfloat16
    )
    grad, loss, rows = head_part(final_rows, head_weight, kernel_order(all_targets))
    return loss[0, 0], head_gradient(grad, rows)


def solution(mesh):
    in_specs = (
        P("seq", "vocab"),
        P("seq"),
        P("seq"),
        P("seq", "vocab"),
        P("vocab"),
        P("vocab"),
        P("vocab", "seq"),
        P("vocab", "seq"),
        P("seq"),
        P(("seq", "vocab"), None),
    )
    out_specs = (P(), P(("seq", "vocab"), None))
    return jax.shard_map(body, mesh=mesh, in_specs=in_specs, out_specs=out_specs, check_vma=False)
```

time: 554 us -> 362 us (0.65)
  blocking collectives: 288 us -> 125 us
  waiting for transfers between devices: 190 us -> 99 us
  Pallas kernels: 0 us -> 85.7 us
  matrix products: 33 us -> 4.53 us
    pallas_call x0 -> x2, Pallas kernels: none -> 85.7 us  [the longest x1 71.1 us: head_part(): pl.pallas_call(head_kernel, out_shape=(jax.ShapeDtypeStruct((512, 1024),...]
    all_gather x1 -> x0, waiting for transfers between devices: 72.1 us -> none  [body(): block_rows = lax.all_gather(wide_rows, 'vocab', axis=0, tiled=True)]
    pmax x1 -> x0, blocking collectives: 65.7 us -> none  [body(): row_peak = lax.pmax(local_peak, ('seq', 'vocab'))]
    psum x1 -> x0, blocking collectives: 63.2 us -> none  [body(): lax.psum((jnp.sum(jnp.exp(scores - row_peak[:, None]), axis=1), local_cho...]
    all_gather x1 -> x0, blocking collectives: 35.3 us -> none  [body(): wide_rows = lax.all_gather(final_rows, 'seq', axis=1, tiled=True)]
    dot_general x2 -> x0, matrix products: 28.5 us -> none  [the longest x1 15.3 us: body(): lax.dot_general(logit_grad, block_rows, (((0,), (0,)), ((), ())), preferr...]
    reduce_scatter x1, waiting for transfers between devices: 61 us -> 42 us  [body(): lax.psum_scatter(jnp.dot(normed_hidden, proj_hidden, preferred_element_ty...]
    unnamed x17 -> x19, local copies, waits for them, and re-layouts: 11.6 us -> 13.5 us
  transfers between devices with their start and end apart: 3 -> 2, of which waited for: 3 -> 2; matrix products, arithmetic and copies ran while one was open for 0% -> 1% of each run, Pallas kernels for 0% -> 0%
where the time goes in v1:
time: 362 us; the launch traced here: 361 us
  blocking collectives  125 us (35%)
  waiting for transfers between devices  99 us (27%)
  Pallas kernels  85.7 us (24%)
  local copies, waits for them, and re-layouts  22.8 us (6%)
  between operations  16 us (4%)
  other arithmetic  7.38 us (2%)
  matrix products  4.53 us (1%)
    pallas_call x1, Pallas kernels, head_part(): pl.pallas_call(head_kernel, out_shape=(jax.ShapeDtypeStruct((512, 1024),...  71.1 us
    psum x1, waiting for transfers between devices, body(): embedded = lax.psum(looked_up, 'seq').astype(jnp.float32)  56.9 us
    reduce_scatter x1, waiting for transfers between devices, body(): lax.psum_scatter(jnp.dot(normed_hidden, proj_hidden, preferred_element_ty...  42 us
    all_gather x1, blocking collectives, body(): lax.all_gather(hidden, 'seq', axis=0, tiled=True).astype(jnp.float32)  35 us
    psum x1, blocking collectives, body(): lax.psum((jnp.sum(all_hidden * all_hidden, axis=1), jnp.sum(embedded * em...  32.9 us
    all_gather x1, blocking collectives, body(): lax.all_gather(next_ids, 'seq', axis=0, tiled=True)  20.8 us
    psum x1, blocking collectives, body(): proj_sq = lax.psum(jnp.sum(projected * projected, axis=1), 'seq')  20.1 us
    all_gather x1, blocking collectives, body(): lax.all_gather(targets, 'seq', axis=0, tiled=True)  16.3 us
  transfers between devices with their start and end apart: 2, of which 2 were waited for; matrix products, arithmetic and copies ran while one was open for 1% of the time, Pallas kernels for 0%

profile of v1, /device:TPU:1, one launch (start us, length us, event | category | flops | bytes accessed | tf_op | source)
XLA Modules:
  0.0 360.6 jit_solution(361965215808356052)
XLA Ops:
  7.2 0.0 copy-start
  7.2 0.0 all-reduce.3.cloned.1.call-start
  7.2 20.8 %all-gather = s32[8,1,128]{2,1,0:T(1,128)S(1)} all-gather(s32[1,1,128]{2,1,0:T(1,128)} %bitcast.25), channel_id=1, replica_groups=mesh['seq'=8,'vocab'=16] {'seq'}, dimensions={0}, use_global_device_ids=true | all-gather | bytes 4608 | tf_op jit(solution)/shard_map/all_gather | solution.py:373
  28.1 11.6 %copy.16 = bf16[8192,448]{1,0:T(8,128)(2,1)} copy(bf16[8192,448]{0,1:T(8,128)(2,1)} %param.13) | data formatting | bytes 14680064 | tf_op args[3]
  39.7 8.4 %gather_fusion = bf16[1024,448]{1,0:T(8,128)(2,1)S(1)} fusion(bf16[8192,448]{1,0:T(8,128)(2,1)} %copy.16, s32[1024]{0:T(1024)S(1)} %fusion.13), kind=kCustom, calls=%fused_computation | custom fusion | bytes 1839104 | tf_op jit(solution)/shard_map/jit(_take)/gather | solution.py:379
  48.1 0.0 copy-start.4
  48.2 1.6 select_select_fusion
  49.8 0.0 copy-start.8
  49.8 0.0 all-reduce.3.cloned.1.call-update
  49.8 0.0 reduce-scatter.2.cloned.1.call-start
  49.8 0.0 copy-done.4
  49.8 35.0 %all_gather.9 = bf16[1024,448]{0,1:T(8,128)(2,1)S(1)} all-gather(bf16[128,448]{0,1:T(8,128)(2,1)S(1)} %copy-done.4), channel_id=1, replica_groups=mesh['seq'=8,'vocab'=16] {'seq'}, dimensions={0}, use_global_device_ids=true | all-gather | bytes 1032192 | tf_op jit(solution)/shard_map/all_gather | solution.py:382
  84.9 0.2 fusion.3
  85.1 56.9 %all-reduce.3.cloned.1.call-done = bf16[1024,448]{1,0:T(8,128)(2,1)} async-done(((bf16[1024,448]{1,0:T(8,128)(2,1)}), bf16[1024,448]{1,0:T(8,128)(2,1)}) %all-reduce.3.cloned.1.call-update) | async-done | bytes 917520 | tf_op jit(solution)/shard_map/psum | solution.py:381
  142.0 1.5 fusion
  143.5 32.9 %all-reduce = (f32[1024]{0:T(1024)S(1)}, f32[1024]{0:T(1024)S(1)}) all-reduce(f32[1024]{0:T(1024)S(1)} %fusion.3, f32[1024]{0:T(1024)S(1)} %fusion), channel_id=1, replica_groups=mesh['seq'=8,'vocab'=16] {'vocab'}, use_global_device_ids=true, to_apply=%region_1.2 | all-reduce | flops 2048 | bytes 16384 | tf_op jit(solution)/shard_map/psum | solution.py:383
  176.4 0.0 copy-done
  176.4 0.0 copy-done.8
  176.4 0.0 copy-start.2
  176.4 0.0 copy-start.3
  176.5 0.0 copy-start.6
  176.5 1.4 fusion.9
  177.9 0.0 copy-done.2
  177.9 0.0 copy-done.3
  177.9 0.0 copy-done.6
  177.9 3.1 convolution_add_fusion
  181.0 0.0 copy-start.7
  181.0 0.0 copy-start.5
  181.1 0.0 reduce-scatter.2.cloned.1.call-update
  181.1 0.6 copy-done.7
  181.7 16.3 %all-gather.1 = s32[8,1,128]{2,1,0:T(1,128)S(1)} all-gather(s32[1,1,128]{2,1,0:T(1,128)S(1)} %bitcast.26), channel_id=1, replica_groups=mesh['seq'=8,'vocab'=16] {'seq'}, dimensions={0}, use_global_device_ids=true | all-gather | bytes 4608 | tf_op jit(solution)/shard_map/all_gather | solution.py:374
  198.0 0.5 broadcast.50
  198.5 0.7 reduce.3
  199.2 0.1 reshape.28
  199.3 0.1 slice.11
  199.4 0.1 reshape.29
  199.4 0.1 reshape.30
  199.5 0.6 add_bitcast_fusion.target_ref
  200.1 42.0 %reduce-scatter.2.cloned.1.call-done = f32[64,896]{1,0:T(8,128)} async-done(((f32[1024,896]{1,0:T(8,128)}), f32[64,896]{1,0:T(8,128)}) %reduce-scatter.2.cloned.1.call-update) | async-done | bytes 229392 | tf_op jit(solution)/shard_map/reduce_scatter | solution.py:392
  242.2 1.1 multiply_reduce_fusion
  243.2 20.1 %psum.31 = f32[64]{0:T(128)S(1)} all-reduce(f32[64]{0:T(128)S(1)} %multiply_reduce_fusion), channel_id=1, replica_groups=mesh['seq'=8,'vocab'=16] {'seq'}, use_global_device_ids=true, to_apply=%region_7.8 | all-reduce | flops 64 | bytes 512 | tf_op jit(solution)/shard_map/psum | solution.py:399
  263.4 0.0 copy-done.5
  263.4 1.7 multiply_convert_fusion.block_ref
  265.1 71.1 %shard_map.113 = (bf16[512,1024]{1,0:T(8,128)(2,1)}, f32[1,1]{1,0:T(1,128)}, bf16[4,4,4,2,64,896]{5,4,3,2,1,0:T(8,128)(2,1)}) custom-call(bf16[64,896]{1,0:T(8,128)(2,1)} %multiply_convert_fusion.block_ref, bf16[512,7168]{1,0:T(8,128)(2,1)} %head_ref.1, s32[8,128]{1,0:T(8,128)} %add_bitcast_fusion.target_ref), custom_call_target="tpu_custom_call" | custom-call | tf_op jit(solution)/shard_map/pallas_call | solution.py:291
  336.2 0.0 copy-start.1
  336.2 1.2 copy-done.1
  337.4 14.6 %shard_map.114 = bf16[512,7168]{1,0:T(8,128)(2,1)} custom-call(bf16[512,1024]{1,0:T(8,128)(2,1)S(1)} %copy-done.1, bf16[4,4,4,2,64,896]{5,4,3,2,1,0:T(8,128)(2,1)} %get-tuple-element.7.rows_ref), custom_call_target="tpu_custom_call" | custom-call | tf_op jit(solution)/shard_map/pallas_call | solution.py:340
  (6 shorter events, 0.1 us)
Async XLA Ops:
  7.2 169.3 %copy-start = (bf16[448,896]{1,0:T(8,128)(2,1)S(1)}, bf16[448,896]{1,0:T(8,128)(2,1)}, u32[]{:S(2)}) copy-start(bf16[448,896]{1,0:T(8,128)(2,1)} %param.16) | copy-start | bytes 2408452
  7.2 134.8 %all-reduce.3.cloned.1.call-start = ((), (), s32[]{:S(2)}) async-start(), calls=%async_computation.1 | async-start | bytes 2097152 | tf_op jit(solution)/shard_map/psum | solution.py:381
  48.1 1.7 copy-start.4
  49.8 126.7 %copy-start.8 = (f32[448]{0:T(512)S(1)}, f32[448]{0:T(512)}, u32[]{:S(2)}) copy-start(f32[448]{0:T(512)} %param.14) | copy-start | bytes 5380
  49.8 192.4 %reduce-scatter.2.cloned.1.call-start = ((), (), s32[]{:S(2)}) async-start(), calls=%async_computation.2 | async-start | bytes 3899392 | tf_op jit(solution)/shard_map/reduce_scatter | solution.py:392
  176.4 1.4 copy-start.2
  176.4 1.4 copy-start.3
  176.5 1.4 copy-start.6
  181.0 0.7 copy-start.7
  181.0 82.3 %copy-start.5 = (f32[896]{0:T(1024)S(1)}, f32[896]{0:T(1024)}, u32[]{:S(2)}) copy-start(f32[896]{0:T(1024)} %param.18) | copy-start | bytes 10756
  336.2 1.2 copy-start.1
Sparse Core Ops, SparseCore 0:
  49.9 92.0 all-reduce.2
  181.2 60.9 reduce-scatter.1

commit v2 on v1

--- a/solution.py
+++ b/solution.py
@@ -39,11 +39,282 @@
     pl.semaphore_wait(barrier, len(peers))
 
 
-def head_kernel(
-    block_ref, head_ref, target_ref, grad_ref, loss_ref, rows_out,
-    rows, head, scores, stats, vstats, sstats,
-    ring_send, ring_recv, pair_send, pair_recv, stat_send, stat_recv, local_sem, out_sem,
+def row_to_columns(row):
+    return jnp.transpose(jnp.broadcast_to(row, (128, 128)))
+
+
+def lane_sums(values):
+    total = jnp.zeros((values.shape[0], 128), jnp.float32)
+    for first in range(0, values.shape[1], 128):
+        total += values[:, first : first + 128] * values[:, first : first + 128]
+    return total
+
+
+def join_kernel(
+    hidden_ref, ids_ref, targets_ref, table_ref, gain_hidden_ref, gain_embed_ref,
+    proj_hidden_ref, proj_embed_ref, gain_final_ref,
+    table, tokens, hidden, embed, gains, parts, relay_in, sums_in, x_out, x_in,
+    squares, square_slots, projected, pair_in, z_out, z_relay, z_in, xl_out, xl_in,
+    final_squares, final_slots, s_send, s_recv, v_send, v_recv, q_send, q_recv, table_sem,
+    vocab_peers, seq_peers, finish_block,
 ):
+    pos, core = coordinates()
+    x, y, z = pos
+    seq, vocab = lax.axis_index("seq"), lax.axis_index("vocab")
+    x_hi, x_lo = lax.div(x, 2), lax.rem(x, 2)
+    y_up, y_down, y_far = lax.rem(y + 1, 4), lax.rem(y + 3, 4), lax.rem(y + 2, 4)
+    z_up, z_down, z_far = lax.rem(z + 1, 4), lax.rem(z + 3, 4), lax.rem(z + 2, 4)
+    to_y_up, to_y_down = (2 * y_up + x_hi, vocab), (2 * y_down + x_hi, vocab)
+    to_x = (2 * y + 1 - x_hi, vocab)
+    inner = 2 * x_lo + core
+    to_z_up, to_z_down = (seq, 4 * z_up + inner), (seq, 4 * z_down + inner)
+    to_pair, to_xl = (seq, 4 * z + 2 * x_lo + 1 - core), (seq, 4 * z + 2 * (1 - x_lo) + core)
+    sent = []
+
+    def copy_to(source, there, sems, number, to):
+        copy = pltpu.make_async_remote_copy(
+            src_ref=source, dst_ref=there, send_sem=sems[0].at[number], recv_sem=sems[1].at[number],
+            device_id=to, device_id_type=MESH,
+        )
+        copy.start()
+        sent.append(copy)
+
+    def arrived(place, sems, number, to):
+        pltpu.make_async_remote_copy(
+            src_ref=place, dst_ref=place, send_sem=sems[0].at[number], recv_sem=sems[1].at[number],
+            device_id=to, device_id_type=MESH,
+        ).wait_recv()
+
+    s_sems, v_sems, q_sems = (s_send, s_recv), (v_send, v_recv), (q_send, q_recv)
+
+    def all_to_all(buffer, me, peers, sems, base):
+        for i, peer in enumerate(peers):
+            copy_to(buffer.at[me], buffer.at[me], sems, base + i, peer)
+
+    def all_from_all(buffer, me, peers, sems, base):
+        count = len(peers) + 1
+        for i, peer in enumerate(peers):
+            arrived(buffer.at[lax.rem(me - (i + 1) + count, count)], sems, base + i, peer)
+
+    table_copy = pltpu.make_async_copy(table_ref, table, table_sem.at[0])
+    table_copy.start()
+    tokens[seq, 0:1] = ids_ref[...]
+    tokens[seq, 1:2] = targets_ref[...]
+    all_to_all(tokens, seq, seq_peers, q_sems, 0)
+    hidden[seq] = hidden_ref[...]
+    copy_to(hidden.at[seq], hidden.at[seq], s_sems, 0, to_x)
+    copy_to(hidden.at[seq], hidden.at[seq], s_sems, 1, to_y_up)
+    copy_to(hidden.at[seq], hidden.at[seq], s_sems, 2, to_y_down)
+    for which, gain_ref in enumerate((gain_hidden_ref, gain_embed_ref)):
+        for first in range(0, 448, 128):
+            row = gain_ref[:, first : min(first + 128, 448)]
+            if first == 384:
+                row = jnp.concatenate([row, jnp.zeros((1, 64), jnp.float32)], axis=1)
+            gains[which, first : min(first + 128, 448)] = row_to_columns(row)[: min(448 - first, 128)]
+    all_from_all(tokens, seq, seq_peers, q_sems, 0)
+    table_copy.wait()
+
+    def look_up(y_at):
+        ids = jnp.concatenate([tokens[2 * y_at, 0:1], tokens[2 * y_at + 1, 0:1]], axis=1) - seq * 8192
+        total = jnp.zeros((448, 256), jnp.float32)
+        for first in range(0, 8192, 1024):
+            entries = lax.broadcasted_iota(jnp.int32, (1024, 256), 0) + first
+            chosen = jnp.where(entries == ids, 1.0, 0.0).astype(jnp.bfloat16)
+            total += jnp.dot(table[:, first : first + 1024], chosen, preferred_element_type=jnp.float32)
+        return total.astype(jnp.bfloat16)
+
+    def store_part(y_at, columns):
+        for i in range(2):
+            parts[y_at, i] = columns[:, 128 * i : 128 * i + 128]
+
+    store_part(y_far, look_up(y_far))
+    copy_to(parts.at[y_far, 0], relay_in.at[0], s_sems, 7, to_y_up)
+    copy_to(parts.at[y_far, 1], relay_in.at[1], s_sems, 8, to_y_down)
+
+    other = 2 * y + 1 - x_hi
+    arrived(hidden.at[other], s_sems, 0, to_x)
+    copy_to(hidden.at[other], hidden.at[other], s_sems, 3, to_y_up)
+    copy_to(hidden.at[other], hidden.at[other], s_sems, 4, to_y_down)
+
+    store_part(y_up, look_up(y_up))
+    arrived(relay_in.at[0], s_sems, 7, to_y_down)
+    parts[y_up, 0] += relay_in[0]
+    copy_to(parts.at[y_up], sums_in.at[0], s_sems, 9, to_y_up)
+
+    below, above = 2 * y_down + x_hi, 2 * y_up + x_hi
+    other_below, other_above = 2 * y_down + 1 - x_hi, 2 * y_up + 1 - x_hi
+    far, other_far = 2 * y_far + x_hi, 2 * y_far + 1 - x_hi
+    arrived(hidden.at[below], s_sems, 1, to_y_down)
+    copy_to(hidden.at[below], hidden.at[below], s_sems, 5, to_y_up)
+
+    store_part(y_down, look_up(y_down))
+    arrived(relay_in.at[1], s_sems, 8, to_y_up)
+    parts[y_down, 1] += relay_in[1]
+    copy_to(parts.at[y_down], sums_in.at[1], s_sems, 10, to_y_down)
+
+    arrived(hidden.at[other_above], s_sems, 4, to_y_up)
+    copy_to(hidden.at[other_above], hidden.at[other_above], s_sems, 6, to_y_down)
+
+    own = look_up(y)
+    arrived(sums_in.at[0], s_sems, 9, to_y_down)
+    arrived(sums_in.at[1], s_sems, 10, to_y_up)
+    for i in range(2):
+        x_out[i] = own[:, 128 * i : 128 * i + 128] + (sums_in[0, i] + sums_in[1, i])
+        copy_to(x_out.at[i], x_in.at[i], s_sems, 11 + i, to_x)
+
+    arrived(hidden.at[above], s_sems, 2, to_y_up)
+    arrived(hidden.at[other_below], s_sems, 3, to_y_down)
+    arrived(hidden.at[far], s_sems, 5, to_y_down)
+    arrived(hidden.at[other_far], s_sems, 6, to_y_up)
+
+    def send_squares(source, which):
+        for i in range(8):
+            values = source[i].astype(jnp.float32)
+            square_slots[which, vocab, i : i + 1] = jnp.sum(values * values, axis=0, keepdims=True)
+        slots = square_slots.at[which]
+        all_to_all(slots, vocab, vocab_peers, v_sems, 15 * which)
+
+    def scales(which):
+        slots = square_slots.at[which]
+        all_from_all(slots, vocab, vocab_peers, v_sems, 15 * which)
+        squares[which] = lax.rsqrt(jnp.sum(slots[...], axis=0) / D + EPSILON)
+
+    def project(source, which, weight_ref, z_at):
+        normed = []
+        for i in range(2):
+            scale = squares[which, pl.ds(2 * z_at + i, 1)]
+            values = source[2 * z_at + i].astype(jnp.float32) * scale * gains[which]
+            normed.append(values.astype(jnp.bfloat16))
+        return lax.dot_general(
+            jnp.concatenate(normed, axis=1), weight_ref[...], (((0,), (0,)), ((), ())),
+            preferred_element_type=jnp.float32,
+        ).reshape(2, 2, 64, 896)
+
+    send_squares(hidden, 0)
+    for i in range(2):
+        arrived(x_in.at[i], s_sems, 11 + i, to_x)
+        place = embed.at[2 * y + i]
+        place[...] = x_out[i] + x_in[i]
+        copy_to(place, place, s_sems, 13 + 2 * i, to_y_up)
+        copy_to(place, place, s_sems, 14 + 2 * i, to_y_down)
+    scales(0)
+    z_order = (z_far, z_up, z_down, z)
+    for k in range(2):
+        projected[k] = project(hidden, 0, proj_hidden_ref, z_order[k])
+    arrived(embed.at[2 * y_down], s_sems, 13, to_y_down)
+    copy_to(embed.at[2 * y_down], embed.at[2 * y_down], s_sems, 17, to_y_up)
+    arrived(embed.at[2 * y_up + 1], s_sems, 16, to_y_up)
+    copy_to(embed.at[2 * y_up + 1], embed.at[2 * y_up + 1], s_sems, 18, to_y_down)
+    for k in range(2, 4):
+        projected[k] = project(hidden, 0, proj_hidden_ref, z_order[k])
+    arrived(embed.at[2 * y_up], s_sems, 14, to_y_up)
+    arrived(embed.at[2 * y_down + 1], s_sems, 15, to_y_down)
+    arrived(embed.at[2 * y_far], s_sems, 17, to_y_down)
+    arrived(embed.at[2 * y_far + 1], s_sems, 18, to_y_up)
+    send_squares(embed, 1)
+    scales(1)
+
+    for k in range(4):
+        projected[k] += project(embed, 1, proj_embed_ref, z_order[k])
+        copy_to(projected.at[k, :, 1 - core], pair_in.at[k], s_sems, 19 + k, to_pair)
+
+    def with_pair(k):
+        arrived(pair_in.at[k], s_sems, 19 + k, to_pair)
+        return projected[k, :, core] + pair_in[k]
+
+    z_out[0] = with_pair(0).astype(jnp.bfloat16)
+    copy_to(z_out.at[0, 0], z_relay.at[0], s_sems, 23, to_z_up)
+    copy_to(z_out.at[0, 1], z_relay.at[1], s_sems, 24, to_z_down)
+    for k, (via, to) in ((1, (to_z_down, to_z_up)), (2, (to_z_up, to_z_down))):
+        both = with_pair(k)
+        arrived(z_relay.at[k - 1], s_sems, 22 + k, via)
+        for i in range(2):
+            handed = both[i] + z_relay[i].astype(jnp.float32) if i == k - 1 else both[i]
+            z_out[k, i] = handed.astype(jnp.bfloat16)
+        copy_to(z_out.at[k], z_in.at[k - 1], s_sems, 24 + k, to)
+    own = with_pair(3)
+    arrived(z_in.at[0], s_sems, 25, to_z_down)
+    arrived(z_in.at[1], s_sems, 26, to_z_up)
+    projected[3, :, core] = own + (z_in[0].astype(jnp.float32) + z_in[1].astype(jnp.float32))
+    xl_out[...] = projected[3, 1 - x_lo, core].astype(jnp.bfloat16)
+    copy_to(xl_out, xl_in, s_sems, 27, to_xl)
+    arrived(xl_in, s_sems, 27, to_xl)
+    total = projected[3, x_lo, core] + xl_in[...].astype(jnp.float32)
+
+    spread = jnp.concatenate([lane_sums(total), jnp.zeros((64, 128), jnp.float32)], axis=0)
+    final_slots[seq] = jnp.broadcast_to(jnp.sum(jnp.transpose(spread), axis=0, keepdims=True), (8, 128))
+    all_to_all(final_slots, seq, seq_peers, q_sems, 7)
+    all_from_all(final_slots, seq, seq_peers, q_sems, 7)
+    scale = lax.rsqrt(jnp.sum(final_slots[...], axis=0)[0:1] / D + EPSILON)
+    finish_block((total * row_to_columns(scale)[0:64, 0:1] * gain_final_ref[...]).astype(jnp.bfloat16))
+    return sent
+
+
+JOIN_SCRATCH = [
+    pltpu.VMEM((448, 8192), jnp.bfloat16),
+    pltpu.VMEM((8, 2, 128), jnp.int32),
+    pltpu.VMEM((8, 448, 128), jnp.bfloat16),
+    pltpu.VMEM((8, 448, 128), jnp.bfloat16),
+    pltpu.VMEM((2, 448, 128), jnp.float32),
+    pltpu.VMEM((4, 2, 448, 128), jnp.bfloat16),
+    pltpu.VMEM((2, 448, 128), jnp.bfloat16),
+    pltpu.VMEM((2, 2, 448, 128), jnp.bfloat16),
+    pltpu.VMEM((2, 448, 128), jnp.bfloat16),
+    pltpu.VMEM((2, 448, 128), jnp.bfloat16),
+    pltpu.VMEM((2, 8, 128), jnp.float32),
+    pltpu.VMEM((2, 16, 8, 128), jnp.float32),
+    pltpu.VMEM((4, 2, 2, 64, 896), jnp.float32),
+    pltpu.VMEM((4, 2, 64, 896), jnp.float32),
+    pltpu.VMEM((3, 2, 64, 896), jnp.bfloat16),
+    pltpu.VMEM((2, 64, 896), jnp.bfloat16),
+    pltpu.VMEM((2, 2, 64, 896), jnp.bfloat16),
+    pltpu.VMEM((64, 896), jnp.bfloat16),
+    pltpu.VMEM((64, 896), jnp.bfloat16),
+    pltpu.VMEM((8, 128), jnp.float32),
+    pltpu.VMEM((8, 8, 128), jnp.float32),
+    pltpu.SemaphoreType.DMA((28,)),
+    pltpu.SemaphoreType.DMA((28,)),
+    pltpu.SemaphoreType.DMA((30,)),
+    pltpu.SemaphoreType.DMA((30,)),
+    pltpu.SemaphoreType.DMA((14,)),
+    pltpu.SemaphoreType.DMA((14,)),
+    pltpu.SemaphoreType.DMA((1,)),
+]
+
+
+def order_targets(tokens, target_ref):
+    natural = tokens[:, 1]
+    turned = {0: natural}
+    lane = lax.broadcasted_iota(jnp.int32, (1, 128), 1)
+    for part, (first, count) in enumerate(ROWS):
+        for group in range(16):
+            vocab = 4 * (group // 2 % 4) + 2 * (group // 8) + group % 2
+            start = 16 * first + count * group
+            done = 0
+            while done < count:
+                place, origin = start + done, 64 * vocab + first + done
+                to, at = divmod(place, 128)
+                size = min(count - done, 128 - at)
+                turn = (at - origin) % 128
+                if turn not in turned:
+                    turned[turn] = pltpu.roll(natural, turn, 1)
+                row = turned[turn][origin // 128 : origin // 128 + 1]
+                if at == 0:
+                    line = row
+                else:
+                    line = jnp.where(lane < at, line, row)
+                if at + size == 128:
+                    target_ref[to : to + 1] = line
+                done += size
+
+
+def whole_kernel(*refs):
+    inputs, (head_ref, grad_ref, loss_ref, rows_out) = refs[:9], refs[9:13]
+    join_scratch = refs[13 : 13 + len(JOIN_SCRATCH)]
+    (
+        rows, head, scores, stats, vstats, sstats, target_ref,
+        ring_send, ring_recv, pair_send, pair_recv, stat_send, stat_recv, local_sem, out_sem,
+    ) = refs[13 + len(JOIN_SCRATCH) :]
     pos, core = coordinates()
     seq, vocab = lax.axis_index("seq"), lax.axis_index("vocab")
     x, y, z = pos
@@ -60,7 +331,11 @@
     across = device(shifted(pos, 0, 1 - 2 * (1 - lax.rem(x, 2))), core)
     greet(vocab_peers + seq_peers + [across])
 
-    rows[x, y, z, core] = block_ref[...]
+    def finish_block(block):
+        rows[x, y, z, core] = block
+
+    sent = join_kernel(*inputs, *join_scratch, vocab_peers, seq_peers, finish_block)
+    order_targets(join_scratch[1], target_ref)
 
     def unit(part, at, axis, half=None):
         index = list(at)
@@ -283,35 +558,37 @@
                 pair(part, number, where, mine, mine).wait_send()
 
     by_core(finish, 0)
+    for copy in sent:
+        copy.wait_send()
     for copy in out_copies:
         copy.wait()
 
 
-def head_part(block, head_weight, targets):
+def whole(*arguments):
     return pl.pallas_call(
-        head_kernel,
+        whole_kernel,
         out_shape=(
             jax.ShapeDtypeStruct((512, 1024), jnp.bfloat16),
             jax.ShapeDtypeStruct((1, 1), jnp.float32),
             jax.ShapeDtypeStruct((4, 4, 4, 2, 64, 896), jnp.bfloat16),
         ),
-        in_specs=[
-            pl.BlockSpec(memory_space=pltpu.VMEM),
-            pl.BlockSpec(memory_space=pl.ANY),
-            pl.BlockSpec(memory_space=pltpu.VMEM),
-        ],
+        in_specs=[pl.BlockSpec(memory_space=pltpu.VMEM)] * 3
+        + [pl.BlockSpec(memory_space=pl.ANY)]
+        + [pl.BlockSpec(memory_space=pltpu.VMEM)] * 5
+        + [pl.BlockSpec(memory_space=pl.ANY)],
         out_specs=(
             pl.BlockSpec(memory_space=pltpu.VMEM),
             pl.BlockSpec(memory_space=pltpu.SMEM),
             pl.BlockSpec(memory_space=pl.ANY),
         ),
-        scratch_shapes=[
+        scratch_shapes=JOIN_SCRATCH + [
             pltpu.VMEM((4, 4, 4, 2, 64, 896), jnp.bfloat16),
             pltpu.VMEM((8, 512, 896), jnp.bfloat16),
             pltpu.VMEM((512, 1024), jnp.float32),
             pltpu.VMEM((3, 8, 128), jnp.float32),
             pltpu.VMEM((16, 3, 8, 128), jnp.float32),
             pltpu.VMEM((8, 3, 8, 128), jnp.float32),
+            pltpu.VMEM((8, 128), jnp.int32),
             pltpu.SemaphoreType.DMA((2, 23)),
             pltpu.SemaphoreType.DMA((2, 23)),
             pltpu.SemaphoreType.DMA((2, 16)),
@@ -322,9 +599,9 @@
             pltpu.SemaphoreType.DMA((8,)),
         ],
         compiler_params=pltpu.CompilerParams(
-            collective_id=2, has_side_effects=True, vmem_limit_bytes=56 * 1024 * 1024
+            collective_id=2, has_side_effects=True, vmem_limit_bytes=60 * 1024 * 1024
         ),
-    )(block, head_weight, targets)
+    )(*arguments)
 
 
 def grad_kernel(grad_ref, rows_ref, out_ref):
@@ -346,14 +623,8 @@
             pl.BlockSpec((2, 1, 4, 2, 64, 896), lambda i: (i % 2, i // 2, 0, 0, 0, 0)),
         ],
         out_specs=pl.BlockSpec((512, 896), lambda i: (0, i)),
-        compiler_params=pltpu.CompilerParams(vmem_limit_bytes=40 * 1024 * 1024),
+        compiler_params=pltpu.CompilerParams(vmem_limit_bytes=60 * 1024 * 1024),
     )(grad, rows)
-
-
-def kernel_order(values):
-    split = values.reshape(4, 2, 2, 64).transpose(1, 0, 2, 3)
-    parts = [split[..., :HIGH].reshape(-1), split[..., HIGH:].reshape(-1)]
-    return jnp.concatenate(parts).reshape(8, 128)
 
 
 def body(
@@ -368,39 +639,18 @@
     gain_final,
     head_weight,
 ):
-    seq_pos = lax.axis_index("seq")
-    all_ids, all_targets = (
-        lax.all_gather(next_ids, "seq", axis=0, tiled=True),
-        lax.all_gather(targets, "seq", axis=0, tiled=True),
+    grad, loss, rows = whole(
+        hidden.T,
+        next_ids[None],
+        targets[None],
+        embed_table.T,
+        gain_hidden[None],
+        gain_embed[None],
+        proj_hidden,
+        proj_embed,
+        gain_final[None],
+        head_weight,
     )
-    table_rows = embed_table.shape[0]
-    local_ids = all_ids - seq_pos * table_rows
-    inside = (local_ids >= 0) & (local_ids < table_rows)
-    looked_up = jnp.take(embed_table, jnp.clip(local_ids, 0, table_rows - 1), axis=0)
-    looked_up = jnp.where(inside[:, None], looked_up, jnp.zeros((), jnp.bfloat16))
-    embedded = lax.psum(looked_up, "seq").astype(jnp.float32)
-    all_hidden = lax.all_gather(hidden, "seq", axis=0, tiled=True).astype(jnp.float32)
-    hidden_sq, embed_sq = lax.psum(
-        (jnp.sum(all_hidden * all_hidden, axis=1), jnp.sum(embedded * embedded, axis=1)), "vocab"
-    )
-    normed_hidden = (all_hidden * lax.rsqrt(hidden_sq / D + EPSILON)[:, None] * gain_hidden).astype(
-        jnp.bfloat16
-    )
-    normed_embed = (embedded * lax.rsqrt(embed_sq / D + EPSILON)[:, None] * gain_embed).astype(
-        jnp.bfloat16
-    )
-    projected = lax.psum_scatter(
-        jnp.dot(normed_hidden, proj_hidden, preferred_element_type=jnp.float32)
-        + jnp.dot(normed_embed, proj_embed, preferred_element_type=jnp.float32),
-        "vocab",
-        scatter_dimension=0,
-        tiled=True,
-    )
-    proj_sq = lax.psum(jnp.sum(projected * projected, axis=1), "seq")
-    final_rows = (projected * lax.rsqrt(proj_sq / D + EPSILON)[:, None] * gain_final).astype(
-        jnp.bfloat16
-    )
-    grad, loss, rows = head_part(final_rows, head_weight, kernel_order(all_targets))
     return loss[0, 0], head_gradient(grad, rows)
 
 

time: 362 us -> 158 us (0.44)
  blocking collectives: 125 us -> 0 us
  waiting for transfers between devices: 99 us -> 0 us
  Pallas kernels: 85.7 us -> 154 us
  local copies, waits for them, and re-layouts: 22.8 us -> 1.27 us
  between operations: 16 us -> 2.4 us
  other arithmetic: 7.38 us -> 0 us
  matrix products: 4.53 us -> 0 us
    all_gather x3 -> x0, blocking collectives: 72.2 us -> none  [the longest x1 35 us: body(): lax.all_gather(hidden, 'seq', axis=0, tiled=True).astype(jnp.float32)]
    pallas_call x1, Pallas kernels: 71.1 us -> 139 us  [whole(): pl.pallas_call(whole_kernel, out_shape=(jax.ShapeDtypeStruct((512, 1024),...]
    psum x1 -> x0, waiting for transfers between devices: 56.9 us -> none  [body(): embedded = lax.psum(looked_up, 'seq').astype(jnp.float32)]
    psum x2 -> x0, blocking collectives: 53 us -> none  [the longest x1 32.9 us: body(): lax.psum((jnp.sum(all_hidden * all_hidden, axis=1), jnp.sum(embedded * em...]
    reduce_scatter x1 -> x0, waiting for transfers between devices: 42 us -> none  [body(): lax.psum_scatter(jnp.dot(normed_hidden, proj_hidden, preferred_element_ty...]
    unnamed x19 -> x0, local copies, waits for them, and re-layouts: 13.5 us -> none
    gather x1 -> x0, local copies, waits for them, and re-layouts: 8.45 us -> none  [body(): jnp.take(embed_table, jnp.clip(local_ids, 0, table_rows - 1), axis=0)]
    dot_general x2 -> x0, matrix products: 4.53 us -> none  [the longest x1 3.15 us: body(): jnp.dot(normed_embed, proj_embed, preferred_element_type=jnp.float32)]
  transfers between devices with their start and end apart: 2 -> 0, of which waited for: 2 -> 0; matrix products, arithmetic and copies ran while one was open for 1% -> 0% of each run, Pallas kernels for 0% -> 0%
where the time goes in v2:
time: 158 us; the launch traced here: 157 us
  Pallas kernels  154 us (97%)
  between operations  2.4 us (2%)
    pallas_call x1, Pallas kernels, whole(): pl.pallas_call(whole_kernel, out_shape=(jax.ShapeDtypeStruct((512, 1024),...  139 us
    pallas_call x1, Pallas kernels, head_gradient(): pl.pallas_call(grad_kernel, out_shape=jax.ShapeDtypeStruct((512, D), jnp....  14.9 us

profile of v2, /device:TPU:1, one launch (start us, length us, event | category | flops | bytes accessed | tf_op | source)
XLA Modules:
  0.0 157.4 jit_solution(17505025833432801369)
XLA Ops:
  0.6 1.3 broadcast_in_dim.19.refs_8_
  1.9 138.8 %shard_map.113 = (bf16[512,1024]{1,0:T(8,128)(2,1)}, f32[1,1]{1,0:T(1,128)}, bf16[4,4,4,2,64,896]{5,4,3,2,1,0:T(8,128)(2,1)}) custom-call(bf16[448,128]{1,0:T(8,128)(2,1)} %bitcast.8, s32[1,128]{1,0:T(1,128)} %bitcast.11, s32[1,128]{1,0:T(1,128)} %bitcast.12, bf16[448,8192]{1,0:T(8,128)(2,1)} %bitcast.7, f32[1,448]{1,0:T(1,128)} %bitcast.9, ...), custom_call_target="tpu_custom_call" | custom-call | tf_op jit(solution)/shard_map/pallas_call | solution.py:568
  140.7 14.9 %shard_map.114 = bf16[512,7168]{1,0:T(8,128)(2,1)} custom-call(bf16[512,1024]{1,0:T(8,128)(2,1)} %get-tuple-element.6.grad_ref, bf16[4,4,4,2,64,896]{5,4,3,2,1,0:T(8,128)(2,1)} %get-tuple-element.7.rows_ref), custom_call_target="tpu_custom_call" | custom-call | tf_op jit(solution)/shard_map/pallas_call | solution.py:617

commit v3 on v1

--- a/solution.py
+++ b/solution.py
@@ -1,3 +1,5 @@
+import functools
+
 import jax
 import jax.numpy as jnp
 from jax import lax
@@ -39,11 +41,263 @@
     pl.semaphore_wait(barrier, len(peers))
 
 
-def head_kernel(
-    block_ref, head_ref, target_ref, grad_ref, loss_ref, rows_out,
-    rows, head, scores, stats, vstats, sstats,
-    ring_send, ring_recv, pair_send, pair_recv, stat_send, stat_recv, local_sem, out_sem,
+def start_copy(sent, source, there, sems, number, to):
+    copy = pltpu.make_async_remote_copy(
+        src_ref=source, dst_ref=there, send_sem=sems[0].at[number], recv_sem=sems[1].at[number],
+        device_id=to, device_id_type=MESH,
+    )
+    copy.start()
+    sent.append(copy)
+
+
+def arrived(place, sems, number, to):
+    pltpu.make_async_remote_copy(
+        src_ref=place, dst_ref=place, send_sem=sems[0].at[number], recv_sem=sems[1].at[number],
+        device_id=to, device_id_type=MESH,
+    ).wait_recv()
+
+
+def all_to_all(copy_to, buffer, me, peers, sems, base):
+    for i, peer in enumerate(peers):
+        copy_to(buffer.at[me], buffer.at[me], sems, base + i, peer)
+
+
+def all_from_all(buffer, me, peers, sems, base):
+    count = len(peers) + 1
+    for i, peer in enumerate(peers):
+        arrived(buffer.at[lax.rem(me - (i + 1) + count, count)], sems, base + i, peer)
+
+
+def greet_all(vocab_peers, seq_peers):
+    pos, core = coordinates()
+    across = device(shifted(pos, 0, 1 - 2 * (1 - lax.rem(pos[0], 2))), core)
+    greet(vocab_peers + seq_peers + [across])
+
+
+def row_to_columns(row):
+    return jnp.transpose(jnp.broadcast_to(row, (128, 128)))
+
+
+def lane_sums(values):
+    total = jnp.zeros((values.shape[0], 128), jnp.float32)
+    for first in range(0, values.shape[1], 128):
+        total += values[:, first : first + 128] * values[:, first : first + 128]
+    return total
+
+
+def join_kernel(
+    hidden_ref, ids_ref, targets_ref, table_ref, gain_hidden_ref, gain_embed_ref,
+    proj_hidden_ref, proj_embed_ref, gain_final_ref,
+    table, tokens, hidden, embed, gains, parts, sums_in, square_slots, scale_slots,
+    projected, pair_in, z_out, z_in,
+    h_send, h_recv, r_send, r_recv, g_send, g_recv, v_send, v_recv, q_send, q_recv,
+    p_send, p_recv, z_send, z_recv, table_sem,
+    vocab_peers, seq_peers,
 ):
+    pos, core = coordinates()
+    x, y, z = pos
+    seq, vocab = lax.axis_index("seq"), lax.axis_index("vocab")
+    x_hi, x_lo = lax.div(x, 2), lax.rem(x, 2)
+    y_up, y_down = lax.rem(y + 1, 4), lax.rem(y + 3, 4)
+    to_y_up, to_y_down = (2 * y_up + x_hi, vocab), (2 * y_down + x_hi, vocab)
+    to_x = (2 * y + 1 - x_hi, vocab)
+    to_pair = (seq, 4 * z + 2 * x_lo + 1 - core)
+    sent = []
+    copy_to = functools.partial(start_copy, sent)
+    h_sems, r_sems, g_sems = (h_send, h_recv), (r_send, r_recv), (g_send, g_recv)
+    v_sems, q_sems = (v_send, v_recv), (q_send, q_recv)
+    p_sems, z_sems = (p_send, p_recv), (z_send, z_recv)
+
+    table_copy = pltpu.make_async_copy(table_ref, table, table_sem.at[0])
+    table_copy.start()
+    tokens[seq, 0:1] = ids_ref[...]
+    tokens[seq, 1:2] = targets_ref[...]
+    greet_all(vocab_peers, seq_peers)
+    all_to_all(copy_to, tokens, seq, seq_peers, q_sems, 0)
+    hidden[seq] = hidden_ref[...]
+    copy_to(hidden.at[seq], hidden.at[seq], h_sems, 0, to_x)
+    copy_to(hidden.at[seq], hidden.at[seq], h_sems, 1, to_y_up)
+    copy_to(hidden.at[seq], hidden.at[seq], h_sems, 2, to_y_down)
+
+    def start_scale(which, block):
+        values = block.astype(jnp.float32)
+        total = jnp.sum(values * values, axis=0, keepdims=True)
+        square_slots[which, vocab] = jnp.broadcast_to(total, (8, 128))
+        all_to_all(copy_to, square_slots.at[which], vocab, vocab_peers, v_sems, 15 * which)
+
+    def spread_scale(which):
+        all_from_all(square_slots.at[which], vocab, vocab_peers, v_sems, 15 * which)
+        total = jnp.sum(square_slots[which], axis=0)
+        scale_slots[which, seq] = lax.rsqrt(total / D + EPSILON)
+        all_to_all(copy_to, scale_slots.at[which], seq, seq_peers, q_sems, 7 + 7 * which)
+
+    def end_scale(which):
+        all_from_all(scale_slots.at[which], seq, seq_peers, q_sems, 7 + 7 * which)
+
+    start_scale(0, hidden_ref[...])
+    for which, gain_ref in enumerate((gain_hidden_ref, gain_embed_ref)):
+        for first in range(0, 448, 128):
+            row = gain_ref[:, first : min(first + 128, 448)]
+            if first == 384:
+                row = jnp.concatenate([row, jnp.zeros((1, 64), jnp.float32)], axis=1)
+            gains[which, first : min(first + 128, 448)] = row_to_columns(row)[: min(448 - first, 128)]
+    all_from_all(tokens, seq, seq_peers, q_sems, 0)
+    table_copy.wait()
+
+    def look_up(y_at):
+        ids = jnp.concatenate([tokens[2 * y_at, 0:1], tokens[2 * y_at + 1, 0:1]], axis=1) - seq * 8192
+        total = jnp.zeros((448, 256), jnp.float32)
+        for first in range(0, 8192, 1024):
+            entries = lax.broadcasted_iota(jnp.int32, (1024, 256), 0) + first
+            chosen = jnp.where(entries == ids, 1.0, 0.0).astype(jnp.bfloat16)
+            total += jnp.dot(table[:, first : first + 1024], chosen, preferred_element_type=jnp.float32)
+        return total.astype(jnp.bfloat16)
+
+    def near_or_other(e):
+        return x_hi if e == 0 else 1 - x_hi
+
+    def seq_at(number):
+        return 2 * lax.rem(y + number // 2, 4) + near_or_other(number % 2)
+
+    def look_up_and_send(dy):
+        y_at = lax.rem(y + dy, 4)
+        found = look_up(y_at)
+        for i in range(2):
+            parts[y_at, i] = found[:, 128 * i : 128 * i + 128]
+        for e in range(2):
+            number = 2 * dy + e
+            if number:
+                source = parts.at[y_at, near_or_other(e)]
+                copy_to(source, sums_in.at[number], r_sems, number, (seq_at(number), vocab))
+
+    other = 2 * y + 1 - x_hi
+    below, above = 2 * y_down + x_hi, 2 * y_up + x_hi
+    other_below, other_above = 2 * y_down + 1 - x_hi, 2 * y_up + 1 - x_hi
+    far, other_far = seq_at(4), seq_at(5)
+    look_up_and_send(2)
+    arrived(hidden.at[other], h_sems, 0, to_x)
+    copy_to(hidden.at[other], hidden.at[other], h_sems, 3, to_y_up)
+    copy_to(hidden.at[other], hidden.at[other], h_sems, 4, to_y_down)
+    arrived(hidden.at[below], h_sems, 1, to_y_down)
+    copy_to(hidden.at[below], hidden.at[below], h_sems, 5, to_y_up)
+    spread_scale(0)
+    look_up_and_send(1)
+    look_up_and_send(3)
+    arrived(hidden.at[other_above], h_sems, 4, to_y_up)
+    copy_to(hidden.at[other_above], hidden.at[other_above], h_sems, 6, to_y_down)
+    look_up_and_send(0)
+    total = parts[y, x_hi]
+    for number in range(1, 8):
+        arrived(sums_in.at[number], r_sems, number, to_x)
+        total += sums_in[number]
+    embed[seq] = total
+    for number in range(1, 8):
+        copy_to(embed.at[seq], embed.at[seq], g_sems, number, (seq_at(number), vocab))
+    start_scale(1, total)
+
+    def project(source, which, weight_ref, z_at):
+        normed = []
+        for i in range(2):
+            values = source[2 * z_at + i].astype(jnp.float32) * scale_slots[which, 2 * z_at + i, 0:1]
+            normed.append((values * gains[which]).astype(jnp.bfloat16))
+        return lax.dot_general(
+            jnp.concatenate(normed, axis=1), weight_ref[...], (((0,), (0,)), ((), ())),
+            preferred_element_type=jnp.float32,
+        ).reshape(2, 2, 64, 896)
+
+    arrived(hidden.at[above], h_sems, 2, to_y_up)
+    arrived(hidden.at[other_below], h_sems, 3, to_y_down)
+    arrived(hidden.at[far], h_sems, 5, to_y_down)
+    arrived(hidden.at[other_far], h_sems, 6, to_y_up)
+    end_scale(0)
+    distances = (2, 1, 3, 0)
+    for k in range(4):
+        projected[k] = project(hidden, 0, proj_hidden_ref, lax.rem(z + distances[k], 4))
+        if k == 1:
+            spread_scale(1)
+    for number in range(1, 8):
+        sender = 2 * lax.rem(y + 4 - number // 2, 4) + near_or_other(number % 2)
+        arrived(embed.at[sender], g_sems, number, to_x)
+    end_scale(1)
+
+    def hand_on(k):
+        arrived(pair_in.at[k], p_sems, k, to_pair)
+        both = projected[k, :, core] + pair_in[k]
+        z_out[k] = both.astype(jnp.bfloat16)
+        dz = distances[k]
+        for e in range(2):
+            number = 2 * dz + e
+            x_at = x_lo if e == 0 else 1 - x_lo
+            if number:
+                to = (seq, 4 * lax.rem(z + dz, 4) + 2 * x_at + core)
+                copy_to(z_out.at[k, x_at], z_in.at[number], z_sems, number, to)
+            else:
+                projected[k, :, core] = both
+
+    for k in range(4):
+        projected[k] += project(embed, 1, proj_embed_ref, lax.rem(z + distances[k], 4))
+        copy_to(projected.at[k, :, 1 - core], pair_in.at[k], p_sems, k, to_pair)
+        if k:
+            hand_on(k - 1)
+    hand_on(3)
+    total = projected[3, x_lo, core]
+    for number in range(1, 8):
+        arrived(z_in.at[number], z_sems, number, to_pair)
+        total += z_in[number].astype(jnp.float32)
+    return total, sent
+
+
+JOIN_SCRATCH = [
+    pltpu.VMEM((448, 8192), jnp.bfloat16),
+    pltpu.VMEM((8, 2, 128), jnp.int32),
+    pltpu.VMEM((8, 448, 128), jnp.bfloat16),
+    pltpu.VMEM((8, 448, 128), jnp.bfloat16),
+    pltpu.VMEM((2, 448, 128), jnp.float32),
+    pltpu.VMEM((4, 2, 448, 128), jnp.bfloat16),
+    pltpu.VMEM((8, 448, 128), jnp.bfloat16),
+    pltpu.VMEM((2, 16, 8, 128), jnp.float32),
+    pltpu.VMEM((2, 8, 8, 128), jnp.float32),
+    pltpu.VMEM((4, 2, 2, 64, 896), jnp.float32),
+    pltpu.VMEM((4, 2, 64, 896), jnp.float32),
+    pltpu.VMEM((4, 2, 64, 896), jnp.bfloat16),
+    pltpu.VMEM((8, 64, 896), jnp.bfloat16),
+    *[pltpu.SemaphoreType.DMA((count,)) for count in (7, 7, 8, 8, 8, 8, 30, 30, 21, 21, 4, 4, 8, 8)],
+    pltpu.SemaphoreType.DMA((1,)),
+]
+
+
+def to_score_order(natural, ordered):
+    turned = {0: natural}
+    lane = lax.broadcasted_iota(jnp.int32, (1, 128), 1)
+    for part, (first, count) in enumerate(ROWS):
+        for group in range(16):
+            vocab = 4 * (group // 2 % 4) + 2 * (group // 8) + group % 2
+            start = 16 * first + count * group
+            done = 0
+            while done < count:
+                place, origin = start + done, 64 * vocab + first + done
+                to, at = divmod(place, 128)
+                size = min(count - done, 128 - at)
+                turn = (at - origin) % 128
+                if turn not in turned:
+                    turned[turn] = pltpu.roll(natural, turn, 1)
+                row = turned[turn][origin // 128 : origin // 128 + 1]
+                if at == 0:
+                    line = row
+                else:
+                    line = jnp.where(lane < at, line, row)
+                if at + size == 128:
+                    ordered[to : to + 1] = line
+                done += size
+
+
+def whole_kernel(*refs):
+    inputs, (head_ref, grad_ref, loss_ref, rows) = refs[:9], refs[9:13]
+    join_scratch = refs[13 : 13 + len(JOIN_SCRATCH)]
+    (
+        head, scores, stats, vocab_stats, seq_stats, targets, scales, final_slots, row_slots,
+        ring_send, ring_recv, pair_send, pair_recv, stat_send, stat_recv, f_send, f_recv, local_sem,
+    ) = refs[13 + len(JOIN_SCRATCH) :]
     pos, core = coordinates()
     seq, vocab = lax.axis_index("seq"), lax.axis_index("vocab")
     x, y, z = pos
@@ -57,10 +311,32 @@
         copy.start()
     vocab_peers = [(seq, lax.rem(vocab + i, 16)) for i in range(1, 16)]
     seq_peers = [(lax.rem(seq + i, 8), vocab) for i in range(1, 8)]
-    across = device(shifted(pos, 0, 1 - 2 * (1 - lax.rem(x, 2))), core)
-    greet(vocab_peers + seq_peers + [across])
-
-    rows[x, y, z, core] = block_ref[...]
+    total, sent = join_kernel(*inputs, *join_scratch, vocab_peers, seq_peers)
+    copy_to = functools.partial(start_copy, sent)
+    f_sems, stat_sems = (f_send, f_recv), (stat_send, stat_recv)
+
+    gain = jnp.concatenate([inputs[8][i : i + 1] for i in range(7)], axis=1)
+    rows[x, y, z, core] = (total * gain).astype(jnp.bfloat16)
+
+    def start_scale():
+        spread = jnp.concatenate([lane_sums(total), jnp.zeros((64, 128), jnp.float32)], axis=0)
+        squares = jnp.sum(jnp.transpose(spread), axis=0, keepdims=True)
+        final_slots[seq] = jnp.broadcast_to(squares, (8, 128))
+        all_to_all(copy_to, final_slots, seq, seq_peers, f_sems, 0)
+
+    def spread_scale():
+        all_from_all(final_slots, seq, seq_peers, f_sems, 0)
+        row_slots[vocab] = lax.rsqrt(jnp.sum(final_slots[...], axis=0) / D + EPSILON)
+        all_to_all(copy_to, row_slots, vocab, vocab_peers, f_sems, 7)
+
+    def end_scale():
+        all_from_all(row_slots, vocab, vocab_peers, f_sems, 7)
+        lane = lax.broadcasted_iota(jnp.int32, (1, 128), 1)
+        natural = []
+        for i in range(8):
+            later = pltpu.roll(row_slots[2 * i + 1], 64, 1)[0:1]
+            natural.append(jnp.where(lane < 64, row_slots[2 * i, 0:1], later))
+        to_score_order(jnp.concatenate(natural, axis=0), scales)
 
     def unit(part, at, axis, half=None):
         index = list(at)
@@ -189,16 +465,6 @@
         else:
             scores[:, columns] += product
 
-    out_copies = []
-
-    def write_out(dy, other):
-        y_at = lax.rem(y + dy + 4, 4)
-        hi_at = lax.rem(x_hi + other, 2)
-        piece = (pl.ds(2 * hi_at, 2), y_at)
-        copy = pltpu.make_async_copy(rows.at[piece], rows_out.at[piece], out_sem.at[len(out_copies)])
-        copy.start()
-        out_copies.append(copy)
-
     ready = {
         4: [(0, 0, 0)],
         6: [(-1, 0, 0), (1, 0, 0)],
@@ -210,67 +476,53 @@
     for step in range(13):
         if step < 12:
             by_core(own_step, step)
-        if step == 3:
+        if step == 0:
+            start_scale()
+            to_score_order(join_scratch[1][:, 1], targets)
+        elif step == 2:
+            spread_scale()
+        elif step == 3:
             for copy in head_copies:
                 copy.wait()
+        elif step == 5:
+            end_scale()
         if step >= 2:
             by_core(pair_step, step - 1)
             for dy, other, part in ready.get(step - 1, []):
                 multiply(dy, other, part)
-                if part == 1:
-                    write_out(dy, other)
 
     first_entry = (seq * 16 + vocab) * 512
     entries = first_entry + lax.broadcasted_iota(jnp.int32, (512, 128), 0)
     for q in range(8):
         columns = slice(128 * q, 128 * q + 128)
-        part = scores[:, columns]
+        part = scores[:, columns] * scales[q : q + 1]
         peak = jnp.max(part, axis=0, keepdims=True)
-        matches = entries == target_ref[q : q + 1, :]
-        chosen = jnp.sum(jnp.where(matches, part, 0.0), axis=0, keepdims=True)
+        matches = entries == targets[q : q + 1]
         powers = jnp.exp(part - peak)
         scores[:, columns] = powers
-        stats[0, q : q + 1, :] = peak
-        stats[1, q : q + 1, :] = jnp.sum(powers, axis=0, keepdims=True)
-        stats[2, q : q + 1, :] = chosen
-
-    def exchange(slots, me, peers, count, base):
-        slots[me] = stats[...]
-        copies = []
-        for i, peer in enumerate(peers):
-            copies.append(pltpu.make_async_remote_copy(
-                src_ref=stats, dst_ref=slots.at[me],
-                send_sem=stat_send.at[base + i], recv_sem=stat_recv.at[base + i],
-                device_id=peer, device_id_type=MESH,
-            ))
-            copies[-1].start()
-        for i in range(len(peers)):
-            sender = lax.rem(me - (i + 1) + count, count)
-            pltpu.make_async_remote_copy(
-                src_ref=stats, dst_ref=slots.at[sender],
-                send_sem=stat_send.at[base + i], recv_sem=stat_recv.at[base + i],
-                device_id=peers[i], device_id_type=MESH,
-            ).wait_recv()
-        for copy in copies:
-            copy.wait_send()
-        peaks = slots[:, 0]
-        top = jnp.max(peaks, axis=0)
-        total = jnp.sum(slots[:, 1] * jnp.exp(peaks - top[None]), axis=0)
-        chosen = jnp.sum(slots[:, 2], axis=0)
-        return top, total, chosen
-
-    own_peak = stats[0]
-    top, total, chosen = exchange(vstats, vocab, vocab_peers, 16, 0)
-    stats[0], stats[1], stats[2] = top, total, chosen
-    top, total, chosen = exchange(sstats, seq, seq_peers, 8, 15)
-    log_total = top + jnp.log(total)
+        stats[0, q : q + 1] = peak + jnp.log(jnp.sum(powers, axis=0, keepdims=True))
+        stats[1, q : q + 1] = jnp.sum(jnp.where(matches, part, 0.0), axis=0, keepdims=True)
+        stats[2, q : q + 1] = peak
+
+    def combine(slots):
+        logs = slots[:, 0]
+        top = jnp.max(logs, axis=0)
+        return top + jnp.log(jnp.sum(jnp.exp(logs - top[None]), axis=0)), jnp.sum(slots[:, 1], axis=0)
+
+    vocab_stats[vocab] = stats[0:2]
+    all_to_all(copy_to, vocab_stats, vocab, vocab_peers, stat_sems, 0)
+    all_from_all(vocab_stats, vocab, vocab_peers, stat_sems, 0)
+    seq_stats[seq, 0], seq_stats[seq, 1] = combine(vocab_stats)
+    all_to_all(copy_to, seq_stats, seq, seq_peers, stat_sems, 15)
+    all_from_all(seq_stats, seq, seq_peers, stat_sems, 15)
+    log_total, chosen = combine(seq_stats)
     loss_ref[0, 0] = jnp.sum(log_total - chosen) / 1024
-    stats[0] = jnp.exp(own_peak - log_total)
+    stats[0] = jnp.exp(stats[2] - log_total)
     for q in range(8):
         columns = slice(128 * q, 128 * q + 128)
-        matches = entries == target_ref[q : q + 1, :]
-        grad = scores[:, columns] * stats[0, q : q + 1, :] - jnp.where(matches, 1.0, 0.0)
-        grad_ref[:, columns] = grad.astype(jnp.bfloat16)
+        matches = entries == targets[q : q + 1]
+        grad = scores[:, columns] * stats[0, q : q + 1] - jnp.where(matches, 1.0, 0.0)
+        grad_ref[:, columns] = (grad * scales[q : q + 1]).astype(jnp.bfloat16)
 
     def finish(mine, _):
         for part in range(2):
@@ -283,53 +535,57 @@
                 pair(part, number, where, mine, mine).wait_send()
 
     by_core(finish, 0)
-    for copy in out_copies:
-        copy.wait()
-
-
-def head_part(block, head_weight, targets):
+    for copy in sent:
+        copy.wait_send()
+
+
+def whole(*arguments):
     return pl.pallas_call(
-        head_kernel,
+        whole_kernel,
         out_shape=(
-            jax.ShapeDtypeStruct((512, 1024), jnp.bfloat16),
+            pltpu.VMEM((512, 1024), jnp.bfloat16),
             jax.ShapeDtypeStruct((1, 1), jnp.float32),
-            jax.ShapeDtypeStruct((4, 4, 4, 2, 64, 896), jnp.bfloat16),
+            pltpu.VMEM((4, 4, 4, 2, 64, 896), jnp.bfloat16),
         ),
-        in_specs=[
-            pl.BlockSpec(memory_space=pltpu.VMEM),
-            pl.BlockSpec(memory_space=pl.ANY),
-            pl.BlockSpec(memory_space=pltpu.VMEM),
-        ],
+        in_specs=[pl.BlockSpec(memory_space=pltpu.VMEM)] * 3
+        + [pl.BlockSpec(memory_space=pl.ANY)]
+        + [pl.BlockSpec(memory_space=pltpu.VMEM)] * 5
+        + [pl.BlockSpec(memory_space=pl.ANY)],
         out_specs=(
             pl.BlockSpec(memory_space=pltpu.VMEM),
             pl.BlockSpec(memory_space=pltpu.SMEM),
-            pl.BlockSpec(memory_space=pl.ANY),
+            pl.BlockSpec(memory_space=pltpu.VMEM),
         ),
-        scratch_shapes=[
-            pltpu.VMEM((4, 4, 4, 2, 64, 896), jnp.bfloat16),
+        scratch_shapes=JOIN_SCRATCH + [
             pltpu.VMEM((8, 512, 896), jnp.bfloat16),
             pltpu.VMEM((512, 1024), jnp.float32),
             pltpu.VMEM((3, 8, 128), jnp.float32),
-            pltpu.VMEM((16, 3, 8, 128), jnp.float32),
-            pltpu.VMEM((8, 3, 8, 128), jnp.float32),
+            pltpu.VMEM((16, 2, 8, 128), jnp.float32),
+            pltpu.VMEM((8, 2, 8, 128), jnp.float32),
+            pltpu.VMEM((8, 128), jnp.int32),
+            pltpu.VMEM((8, 128), jnp.float32),
+            pltpu.VMEM((8, 8, 128), jnp.float32),
+            pltpu.VMEM((16, 8, 128), jnp.float32),
             pltpu.SemaphoreType.DMA((2, 23)),
             pltpu.SemaphoreType.DMA((2, 23)),
             pltpu.SemaphoreType.DMA((2, 16)),
             pltpu.SemaphoreType.DMA((2, 16)),
             pltpu.SemaphoreType.DMA((22,)),
             pltpu.SemaphoreType.DMA((22,)),
-            pltpu.SemaphoreType.DMA((8,)),
+            pltpu.SemaphoreType.DMA((22,)),
+            pltpu.SemaphoreType.DMA((22,)),
             pltpu.SemaphoreType.DMA((8,)),
         ],
         compiler_params=pltpu.CompilerParams(
-            collective_id=2, has_side_effects=True, vmem_limit_bytes=56 * 1024 * 1024
+            collective_id=2, has_side_effects=True, vmem_limit_bytes=44 * 1024 * 1024
         ),
-    )(block, head_weight, targets)
+    )(*arguments)
 
 
 def grad_kernel(grad_ref, rows_ref, out_ref):
-    high = rows_ref[:, 0, :, :, 0:HIGH, :].reshape(16 * HIGH, 896)
-    low = rows_ref[:, 0, :, :, HIGH:64, :].reshape(16 * LOW, 896)
+    y_at, hi_at = lax.div(pl.program_id(0), 2), lax.rem(pl.program_id(0), 2)
+    high = rows_ref[pl.ds(2 * hi_at, 2), y_at, :, :, 0:HIGH, :].reshape(16 * HIGH, 896)
+    low = rows_ref[pl.ds(2 * hi_at, 2), y_at, :, :, HIGH:64, :].reshape(16 * LOW, 896)
     out_ref[...] = (
         jnp.dot(grad_ref[:, : 16 * HIGH], high, preferred_element_type=jnp.float32)
         + jnp.dot(grad_ref[:, 16 * HIGH :], low, preferred_element_type=jnp.float32)
@@ -341,19 +597,10 @@
         grad_kernel,
         out_shape=jax.ShapeDtypeStruct((512, D), jnp.bfloat16),
         grid=(8,),
-        in_specs=[
-            pl.BlockSpec((512, 1024), lambda i: (0, 0)),
-            pl.BlockSpec((2, 1, 4, 2, 64, 896), lambda i: (i % 2, i // 2, 0, 0, 0, 0)),
-        ],
+        in_specs=[pl.BlockSpec(memory_space=pltpu.VMEM)] * 2,
         out_specs=pl.BlockSpec((512, 896), lambda i: (0, i)),
-        compiler_params=pltpu.CompilerParams(vmem_limit_bytes=40 * 1024 * 1024),
-    )(grad, rows)
-
-
-def kernel_order(values):
-    split = values.reshape(4, 2, 2, 64).transpose(1, 0, 2, 3)
-    parts = [split[..., :HIGH].reshape(-1), split[..., HIGH:].reshape(-1)]
-    return jnp.concatenate(parts).reshape(8, 128)
+        compiler_params=pltpu.CompilerParams(vmem_limit_bytes=24 * 1024 * 1024),
+    )(pltpu.with_memory_space_constraint(grad, pltpu.VMEM), pltpu.with_memory_space_constraint(rows, pltpu.VMEM))
 
 
 def body(
@@ -368,39 +615,18 @@
     gain_final,
     head_weight,
 ):
-    seq_pos = lax.axis_index("seq")
-    all_ids, all_targets = (
-        lax.all_gather(next_ids, "seq", axis=0, tiled=True),
-        lax.all_gather(targets, "seq", axis=0, tiled=True),
+    grad, loss, rows = whole(
+        hidden.T,
+        next_ids[None],
+        targets[None],
+        embed_table.T,
+        gain_hidden[None],
+        gain_embed[None],
+        proj_hidden,
+        proj_embed,
+        gain_final.reshape(7, 128),
+        head_weight,
     )
-    table_rows = embed_table.shape[0]
-    local_ids = all_ids - seq_pos * table_rows
-    inside = (local_ids >= 0) & (local_ids < table_rows)
-    looked_up = jnp.take(embed_table, jnp.clip(local_ids, 0, table_rows - 1), axis=0)
-    looked_up = jnp.where(inside[:, None], looked_up, jnp.zeros((), jnp.bfloat16))
-    embedded = lax.psum(looked_up, "seq").astype(jnp.float32)
-    all_hidden = lax.all_gather(hidden, "seq", axis=0, tiled=True).astype(jnp.float32)
-    hidden_sq, embed_sq = lax.psum(
-        (jnp.sum(all_hidden * all_hidden, axis=1), jnp.sum(embedded * embedded, axis=1)), "vocab"
-    )
-    normed_hidden = (all_hidden * lax.rsqrt(hidden_sq / D + EPSILON)[:, None] * gain_hidden).astype(
-        jnp.bfloat16
-    )
-    normed_embed = (embedded * lax.rsqrt(embed_sq / D + EPSILON)[:, None] * gain_embed).astype(
-        jnp.bfloat16
-    )
-    projected = lax.psum_scatter(
-        jnp.dot(normed_hidden, proj_hidden, preferred_element_type=jnp.float32)
-        + jnp.dot(normed_embed, proj_embed, preferred_element_type=jnp.float32),
-        "vocab",
-        scatter_dimension=0,
-        tiled=True,
-    )
-    proj_sq = lax.psum(jnp.sum(projected * projected, axis=1), "seq")
-    final_rows = (projected * lax.rsqrt(proj_sq / D + EPSILON)[:, None] * gain_final).astype(
-        jnp.bfloat16
-    )
-    grad, loss, rows = head_part(final_rows, head_weight, kernel_order(all_targets))
     return loss[0, 0], head_gradient(grad, rows)
 
 

time: 362 us -> 143 us (0.40)
  blocking collectives: 125 us -> 0 us
  waiting for transfers between devices: 99 us -> 0 us
  Pallas kernels: 85.7 us -> 140 us
  local copies, waits for them, and re-layouts: 22.8 us -> 0 us
  between operations: 16 us -> 2.33 us
  other arithmetic: 7.38 us -> 0 us
  matrix products: 4.53 us -> 0 us
    all_gather x3 -> x0, blocking collectives: 72.2 us -> none  [the longest x1 35 us: body(): lax.all_gather(hidden, 'seq', axis=0, tiled=True).astype(jnp.float32)]
    pallas_call x1, Pallas kernels: 71.1 us -> 129 us  [whole(): pl.pallas_call(whole_kernel, out_shape=(pltpu.VMEM((512, 1024), jnp.bfloa...]
    psum x1 -> x0, waiting for transfers between devices: 56.9 us -> none  [body(): embedded = lax.psum(looked_up, 'seq').astype(jnp.float32)]
    psum x2 -> x0, blocking collectives: 53 us -> none  [the longest x1 32.9 us: body(): lax.psum((jnp.sum(all_hidden * all_hidden, axis=1), jnp.sum(embedded * em...]
    reduce_scatter x1 -> x0, waiting for transfers between devices: 42 us -> none  [body(): lax.psum_scatter(jnp.dot(normed_hidden, proj_hidden, preferred_element_ty...]
    unnamed x19 -> x0, local copies, waits for them, and re-layouts: 13.5 us -> none
    gather x1 -> x0, local copies, waits for them, and re-layouts: 8.45 us -> none  [body(): jnp.take(embed_table, jnp.clip(local_ids, 0, table_rows - 1), axis=0)]
    dot_general x2 -> x0, matrix products: 4.53 us -> none  [the longest x1 3.15 us: body(): jnp.dot(normed_embed, proj_embed, preferred_element_type=jnp.float32)]
  transfers between devices with their start and end apart: 2 -> 0, of which waited for: 2 -> 0; matrix products, arithmetic and copies ran while one was open for 1% -> 0% of each run, Pallas kernels for 0% -> 0%
where the time goes in v3:
time: 143 us
  Pallas kernels  140 us (98%)
  between operations  2.33 us (2%)
    pallas_call x1, Pallas kernels, whole(): pl.pallas_call(whole_kernel, out_shape=(pltpu.VMEM((512, 1024), jnp.bfloa...  129 us
    pallas_call x1, Pallas kernels, head_gradient(): pl.pallas_call(grad_kernel, out_shape=jax.ShapeDtypeStruct((512, D), jnp....  11.1 us

profile of v3, /device:TPU:1, one launch (start us, length us, event | category | flops | bytes accessed | tf_op | source)
XLA Modules:
  0.0 142.6 jit_solution(2974590230991926844)
XLA Ops:
  0.6 129.2 %shard_map.113 = (bf16[512,1024]{1,0:T(8,128)(2,1)S(1)}, f32[1,1]{1,0:T(1,128)}, bf16[4,4,4,2,64,896]{5,4,3,2,1,0:T(8,128)(2,1)S(1)}) custom-call(bf16[448,128]{1,0:T(8,128)(2,1)} %bitcast.9, s32[1,128]{1,0:T(1,128)} %bitcast.13, s32[1,128]{1,0:T(1,128)} %bitcast.14, bf16[448,8192]{1,0:T(8,128)(2,1)} %bitcast.8, f32[1,448]{1,0:T(1,128)} %bitcast.11, ...), custom_call_target="tpu_custom_call" | custom-call | tf_op jit(solution)/shard_map/pallas_call | solution.py:543
  129.8 11.1 %shard_map.114 = bf16[512,7168]{1,0:T(8,128)(2,1)} custom-call(bf16[512,1024]{1,0:T(8,128)(2,1)S(1)} %get-tuple-element.6.grad_ref, bf16[4,4,4,2,64,896]{5,4,3,2,1,0:T(8,128)(2,1)S(1)} %get-tuple-element.7.rows_ref), custom_call_target="tpu_custom_call" | custom-call | tf_op jit(solution)/shard_map/pallas_call | solution.py:596

commit v4 on v3

--- a/solution.py
+++ b/solution.py
@@ -10,9 +10,116 @@
 MESH = pl.DeviceIdType.MESH
 D = 7168
 EPSILON = 1e-06
-HIGH, LOW = 48, 16
-ORDERS = (((2, 0, 1), (0, 1, 2)), ((2, 1, 0), (1, 0, 2)))
-ROWS = ((0, HIGH), (HIGH, LOW))
+COLUMNS = ((0, 640), (640, 256))
+ORDERS = (((0, 2, 1), (0, 1, 2)), ((1, 2, 0), (1, 0, 2)))
+OUTSTANDING = 2
+NEAR_Z = ((0, 3), (1, 2))
+SCHEDULE = (
+    (
+        (9, 261, 2, 254, 7, 259, 45, 14, 189, 62),
+        (9, 261, 2, 254, 7, 259, 45, 14, 189, 62),
+        (64,),
+    ),
+    (
+        (260, 252, 44, 12, 29, 237, 205, 110, 78, 256, 309, 278),
+        (44, 12, 260, 252, 29, 237, 205, 110, 78, 256, 309, 278),
+        (65,),
+    ),
+    (
+        (8, 0, 188, 60, 26, 273, 201, 266, 74, 4, 57, 193, 66, 236, 204, 108, 76, 125, 70, 18, 197, 174, 22, 28, 200,
+         72, 49, 53, 141, 94, 221, 138, 272, 264, 24),
+        (188, 60, 8, 0, 26, 273, 125, 266, 74, 4, 57, 201, 66, 236, 204, 108, 76, 193, 70, 18, 197, 174, 22, 28, 124,
+         72, 49, 53, 141, 94, 221, 138, 272, 264, 24),
+        (66,),
+    ),
+    (
+        (192, 64, 276, 269, 90, 42, 217, 290, 308, 56, 124, 68, 122, 134, 196, 172, 321, 313, 129),
+        (200, 64, 276, 269, 90, 42, 217, 290, 308, 192, 68, 56, 134, 122, 196, 172, 321, 313, 129),
+        (32, 36),
+    ),
+    (
+        (140, 92, 158, 249, 16, 82, 220, 136, 20, 38, 88, 209, 48, 86, 52, 213, 154, 216, 120, 268, 132, 241, 114),
+        (140, 92, 158, 249, 16, 82, 220, 136, 20, 38, 88, 209, 48, 86, 52, 213, 154, 216, 132, 268, 120, 241, 114),
+        (0, 4),
+    ),
+    (
+        (245, 282, 40, 118, 128, 156, 248, 33, 293, 286, 233, 80, 106, 185, 208, 84, 150, 212, 288, 145, 152, 320,
+         312, 36, 229, 102, 240, 112, 178, 244, 317, 181, 116),
+        (245, 282, 40, 118, 128, 156, 248, 33, 293, 286, 233, 80, 106, 185, 208, 84, 150, 212, 288, 145, 152, 320,
+         312, 36, 229, 102, 240, 112, 178, 244, 317, 181, 116),
+        (56, 60, 33, 40, 41, 44, 49, 57),
+    ),
+    (
+        (104, 306, 232, 169, 184),
+        (104, 306, 232, 169, 184),
+        (24, 28),
+    ),
+    (
+        (148, 297),
+        (148, 297),
+        (1, 8, 9, 12, 17, 25),
+    ),
+    (
+        (32, 144, 225, 98, 100, 228, 176, 165, 280, 180),
+        (144, 32, 225, 98, 100, 228, 176, 165, 280, 180),
+        (2, 6),
+    ),
+    (
+        (292, 284, 302, 168),
+        (292, 284, 302, 168),
+        (5, 13, 16, 20, 21, 29),
+    ),
+    (
+        (224, 96, 162),
+        (224, 96, 162),
+        (34, 38),
+    ),
+    (
+        (304, 164),
+        (304, 164),
+        (3, 10, 11, 14, 19, 26, 27, 30),
+    ),
+    (
+        (316,),
+        (316,),
+        (58, 62),
+    ),
+    (
+        (296, 160),
+        (296, 160),
+        (37, 45, 48, 52, 53, 61),
+    ),
+    (
+        (300,),
+        (300,),
+        (35, 42, 43, 46, 51, 59),
+    ),
+    (
+        (),
+        (),
+        (7, 15, 18, 22, 23, 31),
+    ),
+    (
+        (),
+        (),
+        (39, 47, 50, 54, 55, 63),
+    ),
+)
+
+
+def received(number):
+    if number < 63:
+        if number < 3:
+            return 0, 1, (number + 1, 0, 0)
+        if number < 15:
+            return 0, 2, ((number - 3) % 4, (number - 3) // 4 + 1, 0)
+        return 0, 3, ((number - 15) % 4, (number - 15) // 4 % 4, (number - 15) // 16 + 1)
+    number -= 63
+    if number < 3:
+        return 1, 1, (number + 1, 0, 0)
+    if number < 6:
+        return 1, 2, (4, number - 2, 0)
+    return 1, 3, (4, (number - 6) % 4, (number - 6) // 4 + 1)
 
 
 def coordinates():
@@ -266,29 +373,11 @@
 ]
 
 
-def to_score_order(natural, ordered):
-    turned = {0: natural}
+def joined(lower, upper, turned):
     lane = lax.broadcasted_iota(jnp.int32, (1, 128), 1)
-    for part, (first, count) in enumerate(ROWS):
-        for group in range(16):
-            vocab = 4 * (group // 2 % 4) + 2 * (group // 8) + group % 2
-            start = 16 * first + count * group
-            done = 0
-            while done < count:
-                place, origin = start + done, 64 * vocab + first + done
-                to, at = divmod(place, 128)
-                size = min(count - done, 128 - at)
-                turn = (at - origin) % 128
-                if turn not in turned:
-                    turned[turn] = pltpu.roll(natural, turn, 1)
-                row = turned[turn][origin // 128 : origin // 128 + 1]
-                if at == 0:
-                    line = row
-                else:
-                    line = jnp.where(lane < at, line, row)
-                if at + size == 128:
-                    ordered[to : to + 1] = line
-                done += size
+    if turned:
+        return jnp.where(lane < 64, pltpu.roll(lower, 64, 1), upper)[0:1]
+    return jnp.where(lane < 64, lower, pltpu.roll(upper, 64, 1))[0:1]
 
 
 def whole_kernel(*refs):
@@ -331,175 +420,136 @@
 
     def end_scale():
         all_from_all(row_slots, vocab, vocab_peers, f_sems, 7)
-        lane = lax.broadcasted_iota(jnp.int32, (1, 128), 1)
-        natural = []
-        for i in range(8):
-            later = pltpu.roll(row_slots[2 * i + 1], 64, 1)[0:1]
-            natural.append(jnp.where(lane < 64, row_slots[2 * i, 0:1], later))
-        to_score_order(jnp.concatenate(natural, axis=0), scales)
-
-    def unit(part, at, axis, half=None):
-        index = list(at)
-        if axis is not None:
-            index[axis] = pl.ds(0, 4) if half is None else pl.ds(2 * half, 2)
-        return index, ROWS[part]
-
-    def ref_of(where, which):
-        index, (first, count) = where
-        return rows.at[index[0], index[1], index[2], which, pl.ds(first, count), :]
-
-    def ring(mine, part, number, where, to):
-        target = device(to, mine)
-        piece = ref_of(where, mine)
+        for c in range(2):
+            for i in range(4):
+                row = joined(row_slots[4 * i + c], row_slots[4 * i + 2 + c], False)
+                scales[4 * c + i : 4 * c + i + 1] = row
+
+    def order_targets():
+        tokens = join_scratch[1]
+        for i in range(4):
+            for c in range(2):
+                lower = jnp.broadcast_to(tokens[2 * i, 1:2], (8, 128))
+                upper = jnp.broadcast_to(tokens[2 * i + 1, 1:2], (8, 128))
+                targets[4 * c + i : 4 * c + i + 1] = joined(lower, upper, c == 1)
+
+    def place(part, core_of, axes, distances):
+        index = [None] * 3
+        for axis, distance in zip(axes, distances):
+            index[axis] = pl.ds(0, 4) if distance == 4 else lax.rem(pos[axis] + distance, 4)
+        first, width = COLUMNS[part]
+        return rows.at[index[0], index[1], index[2], core_of, :, pl.ds(first, width)]
+
+    def ring(mine, code):
+        number, kind = divmod(code, 4)
+        part, stage, distances = received(number)
+        axes = ORDERS[mine][part]
+        by = (0, 1, -1, 2)[kind]
+        if kind:
+            distances = list(distances)
+            distances[stage - 1] = 0 if kind == 3 else (distances[stage - 1] + by) % 4
+        piece = place(part, mine, axes, distances)
+        to = device(shifted(pos, axes[stage - 1], by if kind else 1), mine)
         return pltpu.make_async_remote_copy(
-            src_ref=piece, dst_ref=piece,
-            send_sem=ring_send.at[part, number], recv_sem=ring_recv.at[part, number],
-            device_id=target, device_id_type=MESH,
-        )
-
-    def pair(part, number, where, which, mine):
-        piece = ref_of(where, which)
+            src_ref=piece, dst_ref=piece, send_sem=ring_send.at[number], recv_sem=ring_recv.at[number],
+            device_id=to, device_id_type=MESH,
+        ), (axes[stage - 1], by)
+
+    def pair(mine, which, part, line):
+        piece = place(part, which, ORDERS[which][part], (4, line[0], line[1]))
+        number = 16 * part + 4 * line[1] + line[0]
         return pltpu.make_async_remote_copy(
-            src_ref=piece, dst_ref=piece,
-            send_sem=pair_send.at[part, number], recv_sem=pair_recv.at[part, number],
+            src_ref=piece, dst_ref=piece, send_sem=pair_send.at[number], recv_sem=pair_recv.at[number],
             device_id=device(pos, 1 - mine), device_id_type=MESH,
         )
 
-    def line_units(order, part):
-        a, b, c = order
-        lines = [(1, pos)]
-        lines += [(2, shifted(pos, b, -1)), (2, shifted(pos, b, 1)), (3, shifted(pos, b, 2))]
-        middles = [lines[i][1] for i in range(4)]
-        for j, middle in enumerate(middles):
-            lines += [(4 + j, shifted(middle, c, -1)), (4 + j, shifted(middle, c, 1))]
-        for j, middle in enumerate(middles):
-            lines.append((8 + j, shifted(middle, c, 2)))
-        return [(step, unit(part, at, a)) for step, at in lines]
-
-    def own_step(mine, step):
-        for part in range(2):
-            a, b, c = ORDERS[mine][part]
-
-            def send(number, where, to):
-                ring(mine, part, number, where, to).start()
-
-            def recv(number, where):
-                ring(mine, part, number, where, pos).wait_recv()
-
-            def up(axis):
-                return shifted(pos, axis, 1)
-
-            def down(axis):
-                return shifted(pos, axis, -1)
-
-            middles = [pos, down(b), up(b), shifted(pos, b, 2)]
-
-            def spread(j):
-                send(7 + 4 * j, unit(part, middles[j], a), up(c))
-                send(8 + 4 * j, unit(part, middles[j], a), down(c))
-
-            if step == 0:
-                send(0, unit(part, pos, None), up(a))
-                send(1, unit(part, pos, None), down(a))
-            elif step == 1:
-                recv(0, unit(part, down(a), None))
-                send(2, unit(part, down(a), None), up(a))
-                recv(1, unit(part, up(a), None))
-                recv(2, unit(part, shifted(pos, a, 2), None))
-                send(3, unit(part, pos, a), up(b))
-                send(4, unit(part, pos, a), down(b))
-                spread(0)
-            elif step == 2:
-                recv(3, unit(part, middles[1], a))
-                send(5, unit(part, middles[1], a, 0), up(b))
-                recv(4, unit(part, middles[2], a))
-                send(6, unit(part, middles[2], a, 1), down(b))
-                spread(1)
-                spread(2)
-            elif step == 3:
-                recv(5, unit(part, middles[3], a, 0))
-                recv(6, unit(part, middles[3], a, 1))
-                spread(3)
-            elif step < 8:
-                j = step - 4
-                before, after = shifted(middles[j], c, -1), shifted(middles[j], c, 1)
-                recv(7 + 4 * j, unit(part, before, a))
-                send(9 + 4 * j, unit(part, before, a, 0), up(c))
-                recv(8 + 4 * j, unit(part, after, a))
-                send(10 + 4 * j, unit(part, after, a, 1), down(c))
+    here = [{}, {}]
+    started = [{}, {}]
+    paired = [set(), set()]
+
+    def ring_steps(mine, codes):
+        for code in codes:
+            copy, link = ring(mine, code)
+            if code % 4 == 0:
+                copy.wait_recv()
+                part, _, distances = received(code // 4)
+                line = (part, distances[1], distances[2])
+                count = here[mine].get(line, 1 if line[1:] == (0, 0) else 0)
+                here[mine][line] = count + (4 if distances[0] == 4 else 1)
+                if here[mine][line] == 4:
+                    pair(mine, mine, part, line[1:]).start()
             else:
-                j = step - 8
-                far = shifted(middles[j], c, 2)
-                recv(9 + 4 * j, unit(part, far, a, 0))
-                recv(10 + 4 * j, unit(part, far, a, 1))
-            for number, (when, where) in enumerate(line_units(ORDERS[mine][part], part)):
-                if when == step:
-                    pair(part, number, where, mine, mine).start()
-
-    def pair_step(mine, step):
-        for part in range(2):
-            for number, (when, where) in enumerate(line_units(ORDERS[1 - mine][part], part)):
-                if when == step:
-                    pair(part, number, where, 1 - mine, mine).wait_recv()
-
-    def by_core(action, step):
+                copies = started[mine].setdefault(link, [])
+                if len(copies) >= OUTSTANDING and link[1] != 2:
+                    ring(mine, copies[len(copies) - OUTSTANDING])[0].wait_send()
+                copies.append(code)
+                copy.start()
+
+    def needed(which, part, dy, other, distance):
+        if which == 0:
+            return [(distance, dy) if part == 0 else (dy, distance)]
+        along = (2, 1, 3) if other else (0, 1, 3)
+        return [(distance, dx) if part == 0 else (dx, distance) for dx in along]
+
+    def pair_steps(mine, products):
+        for code in products:
+            part, dy, other, near, which = code // 32, code // 8 % 4, code // 4 % 2, code // 2 % 2, code % 2
+            for distance in NEAR_Z[near]:
+                for line in needed(which, part, dy, other, distance):
+                    if which == mine:
+                        assert here[mine][(part, *line)] == 4
+                    elif (part, line) not in paired[mine]:
+                        paired[mine].add((part, line))
+                        pair(mine, which, part, line).wait_recv()
+
+    def by_core(action, per_core):
         for mine in range(2):
 
             @pl.when(core == mine)
             def _():
-                action(mine, step)
+                action(mine, per_core[mine])
 
     x_hi = lax.div(x, 2)
 
-    def multiply(dy, other, part):
-        y_at = lax.rem(y + dy + 4, 4)
-        hi_at = lax.rem(x_hi + other, 2)
-        first, count = ROWS[part]
-        taken = rows[pl.ds(2 * hi_at, 2), y_at, :, :, pl.ds(first, count), :].reshape(-1, 896)
+    def multiply(code):
+        part, dy, other, near, which = code // 32, code // 8 % 4, code // 4 % 2, code // 2 % 2, code % 2
+        y_at, hi_at = lax.rem(y + dy, 4), lax.rem(x_hi + other, 2)
+        z_at = [lax.rem(z + distance, 4) for distance in NEAR_Z[near]]
+        first, width = COLUMNS[part]
+        columns = pl.ds(first, width)
+        taken = [rows[pl.ds(2 * hi_at, 2), y_at, i, which, :, columns].reshape(128, width) for i in z_at]
         product = lax.dot_general(
-            head[2 * y_at + hi_at], taken, (((1,), (1,)), ((), ())), preferred_element_type=jnp.float32
+            head[2 * y_at + hi_at, :, columns], jnp.concatenate(taken, axis=0), (((1,), (1,)), ((), ())),
+            preferred_element_type=jnp.float32,
         )
-        columns = slice(0, 16 * HIGH) if part == 0 else slice(16 * HIGH, 1024)
-        if (dy, other) == (0, 0):
-            scores[:, columns] = product
-        else:
-            scores[:, columns] += product
-
-    ready = {
-        4: [(0, 0, 0)],
-        6: [(-1, 0, 0), (1, 0, 0)],
-        8: [(0, 1, 0)],
-        9: [(-1, 1, 0)],
-        10: [(2, 0, 0), (1, 1, 0), (0, 0, 1), (-1, 0, 1), (1, 0, 1)],
-        11: [(2, 1, 0), (2, 0, 1), (0, 1, 1), (-1, 1, 1), (1, 1, 1), (2, 1, 1)],
-    }
-    for step in range(13):
-        if step < 12:
-            by_core(own_step, step)
-        if step == 0:
+        for i in range(2):
+            scores[4 * which + z_at[i]] += product[:, 128 * i : 128 * i + 128]
+
+    scores[...] = jnp.zeros_like(scores)
+    for first_core, second_core, products in SCHEDULE:
+        by_core(ring_steps, (first_core, second_core))
+        if products[0] == 64:
             start_scale()
-            to_score_order(join_scratch[1][:, 1], targets)
-        elif step == 2:
+            order_targets()
+        elif products[0] == 65:
             spread_scale()
-        elif step == 3:
+        elif products[0] == 66:
+            end_scale()
             for copy in head_copies:
                 copy.wait()
-        elif step == 5:
-            end_scale()
-        if step >= 2:
-            by_core(pair_step, step - 1)
-            for dy, other, part in ready.get(step - 1, []):
-                multiply(dy, other, part)
+        else:
+            by_core(pair_steps, (products, products))
+            for code in products:
+                multiply(code)
 
     first_entry = (seq * 16 + vocab) * 512
     entries = first_entry + lax.broadcasted_iota(jnp.int32, (512, 128), 0)
     for q in range(8):
-        columns = slice(128 * q, 128 * q + 128)
-        part = scores[:, columns] * scales[q : q + 1]
+        part = scores[q] * scales[q : q + 1]
         peak = jnp.max(part, axis=0, keepdims=True)
         matches = entries == targets[q : q + 1]
         powers = jnp.exp(part - peak)
-        scores[:, columns] = powers
+        scores[q] = powers
         stats[0, q : q + 1] = peak + jnp.log(jnp.sum(powers, axis=0, keepdims=True))
         stats[1, q : q + 1] = jnp.sum(jnp.where(matches, part, 0.0), axis=0, keepdims=True)
         stats[2, q : q + 1] = peak
@@ -521,20 +571,18 @@
     for q in range(8):
         columns = slice(128 * q, 128 * q + 128)
         matches = entries == targets[q : q + 1]
-        grad = scores[:, columns] * stats[0, q : q + 1] - jnp.where(matches, 1.0, 0.0)
+        grad = scores[q] * stats[0, q : q + 1] - jnp.where(matches, 1.0, 0.0)
         grad_ref[:, columns] = (grad * scales[q : q + 1]).astype(jnp.bfloat16)
 
     def finish(mine, _):
+        for (_, by), copies in started[mine].items():
+            for code in copies if by == 2 else copies[-OUTSTANDING:]:
+                ring(mine, code)[0].wait_send()
         for part in range(2):
-            a, b, c = ORDERS[mine][part]
-            sizes = [(pos, None, None)] * 3 + [(pos, a, None)] * 2 + [(pos, a, 0)] * 2
-            sizes += ([(pos, a, None)] * 2 + [(pos, a, 0)] * 2) * 4
-            for number, (at, axis, half) in enumerate(sizes):
-                ring(mine, part, number, unit(part, at, axis, half), pos).wait_send()
-            for number, (_, where) in enumerate(line_units(ORDERS[mine][part], part)):
-                pair(part, number, where, mine, mine).wait_send()
-
-    by_core(finish, 0)
+            for number in range(16):
+                pair(mine, mine, part, (number % 4, number // 4)).wait_send()
+
+    by_core(finish, (None, None))
     for copy in sent:
         copy.wait_send()
 
@@ -558,7 +606,7 @@
         ),
         scratch_shapes=JOIN_SCRATCH + [
             pltpu.VMEM((8, 512, 896), jnp.bfloat16),
-            pltpu.VMEM((512, 1024), jnp.float32),
+            pltpu.VMEM((8, 512, 128), jnp.float32),
             pltpu.VMEM((3, 8, 128), jnp.float32),
             pltpu.VMEM((16, 2, 8, 128), jnp.float32),
             pltpu.VMEM((8, 2, 8, 128), jnp.float32),
@@ -566,10 +614,10 @@
             pltpu.VMEM((8, 128), jnp.float32),
             pltpu.VMEM((8, 8, 128), jnp.float32),
             pltpu.VMEM((16, 8, 128), jnp.float32),
-            pltpu.SemaphoreType.DMA((2, 23)),
-            pltpu.SemaphoreType.DMA((2, 23)),
-            pltpu.SemaphoreType.DMA((2, 16)),
-            pltpu.SemaphoreType.DMA((2, 16)),
+            pltpu.SemaphoreType.DMA((81,)),
+            pltpu.SemaphoreType.DMA((81,)),
+            pltpu.SemaphoreType.DMA((32,)),
+            pltpu.SemaphoreType.DMA((32,)),
             pltpu.SemaphoreType.DMA((22,)),
             pltpu.SemaphoreType.DMA((22,)),
             pltpu.SemaphoreType.DMA((22,)),
@@ -584,11 +632,9 @@
 
 def grad_kernel(grad_ref, rows_ref, out_ref):
     y_at, hi_at = lax.div(pl.program_id(0), 2), lax.rem(pl.program_id(0), 2)
-    high = rows_ref[pl.ds(2 * hi_at, 2), y_at, :, :, 0:HIGH, :].reshape(16 * HIGH, 896)
-    low = rows_ref[pl.ds(2 * hi_at, 2), y_at, :, :, HIGH:64, :].reshape(16 * LOW, 896)
-    out_ref[...] = (
-        jnp.dot(grad_ref[:, : 16 * HIGH], high, preferred_element_type=jnp.float32)
-        + jnp.dot(grad_ref[:, 16 * HIGH :], low, preferred_element_type=jnp.float32)
+    taken = [rows_ref[pl.ds(2 * hi_at, 2), y_at, i, c].reshape(128, 896) for c in range(2) for i in range(4)]
+    out_ref[...] = jnp.dot(
+        grad_ref[...], jnp.concatenate(taken, axis=0), preferred_element_type=jnp.float32
     ).astype(jnp.bfloat16)
 
 

time: 143 us -> 146 us (1.021)
  Pallas kernels: 140 us -> 143 us
    pallas_call x1, Pallas kernels: 129 us -> 132 us  [whole(): pl.pallas_call(whole_kernel, out_shape=(pltpu.VMEM((512, 1024), jnp.bfloa...]
where the time goes in v4:
time: 146 us
  Pallas kernels  143 us (98%)
  between operations  2.33 us (2%)
    pallas_call x1, Pallas kernels, whole(): pl.pallas_call(whole_kernel, out_shape=(pltpu.VMEM((512, 1024), jnp.bfloa...  132 us
    pallas_call x1, Pallas kernels, head_gradient(): pl.pallas_call(grad_kernel, out_shape=jax.ShapeDtypeStruct((512, D), jnp....  11.1 us

profile of v4, /device:TPU:1, one launch (start us, length us, event | category | flops | bytes accessed | tf_op | source)
XLA Modules:
  0.0 145.6 jit_solution(16910433204807672869)
XLA Ops:
  0.6 132.2 %shard_map.113 = (bf16[512,1024]{1,0:T(8,128)(2,1)S(1)}, f32[1,1]{1,0:T(1,128)}, bf16[4,4,4,2,64,896]{5,4,3,2,1,0:T(8,128)(2,1)S(1)}) custom-call(bf16[448,128]{1,0:T(8,128)(2,1)} %bitcast.9, s32[1,128]{1,0:T(1,128)} %bitcast.13, s32[1,128]{1,0:T(1,128)} %bitcast.14, bf16[448,8192]{1,0:T(8,128)(2,1)} %bitcast.8, f32[1,448]{1,0:T(1,128)} %bitcast.11, ...), custom_call_target="tpu_custom_call" | custom-call | tf_op jit(solution)/shard_map/pallas_call | solution.py:591
  132.9 11.1 %shard_map.114 = bf16[512,7168]{1,0:T(8,128)(2,1)} custom-call(bf16[512,1024]{1,0:T(8,128)(2,1)S(1)} %get-tuple-element.6.grad_ref, bf16[4,4,4,2,64,896]{5,4,3,2,1,0:T(8,128)(2,1)S(1)} %get-tuple-element.7.rows_ref), custom_call_target="tpu_custom_call" | custom-call | tf_op jit(solution)/shard_map/pallas_call | solution.py:642

commit v5 on v3

--- a/solution.py
+++ b/solution.py
@@ -88,8 +88,8 @@
 def join_kernel(
     hidden_ref, ids_ref, targets_ref, table_ref, gain_hidden_ref, gain_embed_ref,
     proj_hidden_ref, proj_embed_ref, gain_final_ref,
-    table, tokens, hidden, embed, gains, parts, sums_in, square_slots, scale_slots,
-    projected, pair_in, z_out, z_in,
+    table, tokens, hidden, embed, gains, parts, halves_in, sums_out, sums_in, square_slots, scale_slots,
+    embed_scale, projected, pair_in, z_out, z_in, own,
     h_send, h_recv, r_send, r_recv, g_send, g_recv, v_send, v_recv, q_send, q_recv,
     p_send, p_recv, z_send, z_recv, table_sem,
     vocab_peers, seq_peers,
@@ -106,7 +106,8 @@
     copy_to = functools.partial(start_copy, sent)
     h_sems, r_sems, g_sems = (h_send, h_recv), (r_send, r_recv), (g_send, g_recv)
     v_sems, q_sems = (v_send, v_recv), (q_send, q_recv)
-    p_sems, z_sems = (p_send, p_recv), (z_send, z_recv)
+    p_sems = (p_send, p_recv)
+    mine = 2 * z + x_lo
 
     table_copy = pltpu.make_async_copy(table_ref, table, table_sem.at[0])
     table_copy.start()
@@ -119,22 +120,30 @@
     copy_to(hidden.at[seq], hidden.at[seq], h_sems, 1, to_y_up)
     copy_to(hidden.at[seq], hidden.at[seq], h_sems, 2, to_y_down)
 
-    def start_scale(which, block):
-        values = block.astype(jnp.float32)
+    def start_hidden_scale():
+        values = hidden_ref[...].astype(jnp.float32)
         total = jnp.sum(values * values, axis=0, keepdims=True)
-        square_slots[which, vocab] = jnp.broadcast_to(total, (8, 128))
-        all_to_all(copy_to, square_slots.at[which], vocab, vocab_peers, v_sems, 15 * which)
+        square_slots[0, vocab] = jnp.broadcast_to(total, (8, 128))
+        all_to_all(copy_to, square_slots.at[0], vocab, vocab_peers, v_sems, 0)
+
+    def start_embed_scale():
+        for i in range(8):
+            values = parts[i // 2, i % 2].astype(jnp.float32)
+            square_slots[1, vocab, i : i + 1] = jnp.sum(values * values, axis=0, keepdims=True)
+        all_to_all(copy_to, square_slots.at[1], vocab, vocab_peers, v_sems, 15)
 
     def spread_scale(which):
         all_from_all(square_slots.at[which], vocab, vocab_peers, v_sems, 15 * which)
         total = jnp.sum(square_slots[which], axis=0)
-        scale_slots[which, seq] = lax.rsqrt(total / D + EPSILON)
+        scale_slots[which, seq] = total if which else lax.rsqrt(total / D + EPSILON)
         all_to_all(copy_to, scale_slots.at[which], seq, seq_peers, q_sems, 7 + 7 * which)
 
     def end_scale(which):
         all_from_all(scale_slots.at[which], seq, seq_peers, q_sems, 7 + 7 * which)
-
-    start_scale(0, hidden_ref[...])
+        if which:
+            embed_scale[...] = lax.rsqrt(jnp.sum(scale_slots[1], axis=0) / D + EPSILON)
+
+    start_hidden_scale()
     for which, gain_ref in enumerate((gain_hidden_ref, gain_embed_ref)):
         for first in range(0, 448, 128):
             row = gain_ref[:, first : min(first + 128, 448)]
@@ -164,86 +173,114 @@
         found = look_up(y_at)
         for i in range(2):
             parts[y_at, i] = found[:, 128 * i : 128 * i + 128]
-        for e in range(2):
-            number = 2 * dy + e
-            if number:
-                source = parts.at[y_at, near_or_other(e)]
-                copy_to(source, sums_in.at[number], r_sems, number, (seq_at(number), vocab))
+        copy_to(parts.at[y_at, 1 - x_hi], halves_in.at[dy], r_sems, dy, to_x)
+
+    def sum_and_send(dy):
+        y_at = lax.rem(y + dy, 4)
+        arrived(halves_in.at[dy], r_sems, dy, to_x)
+        total = parts[y_at, x_hi] + halves_in[dy]
+        if dy:
+            sums_out[dy] = total
+            copy_to(sums_out.at[dy], sums_in.at[dy], r_sems, 3 + dy, (2 * y_at + x_hi, vocab))
+        return total
 
     other = 2 * y + 1 - x_hi
     below, above = 2 * y_down + x_hi, 2 * y_up + x_hi
     other_below, other_above = 2 * y_down + 1 - x_hi, 2 * y_up + 1 - x_hi
     far, other_far = seq_at(4), seq_at(5)
     look_up_and_send(2)
+    look_up_and_send(1)
     arrived(hidden.at[other], h_sems, 0, to_x)
     copy_to(hidden.at[other], hidden.at[other], h_sems, 3, to_y_up)
     copy_to(hidden.at[other], hidden.at[other], h_sems, 4, to_y_down)
     arrived(hidden.at[below], h_sems, 1, to_y_down)
     copy_to(hidden.at[below], hidden.at[below], h_sems, 5, to_y_up)
     spread_scale(0)
-    look_up_and_send(1)
     look_up_and_send(3)
+    sum_and_send(2)
+    look_up_and_send(0)
+    sum_and_send(1)
+    start_embed_scale()
     arrived(hidden.at[other_above], h_sems, 4, to_y_up)
     copy_to(hidden.at[other_above], hidden.at[other_above], h_sems, 6, to_y_down)
-    look_up_and_send(0)
-    total = parts[y, x_hi]
-    for number in range(1, 8):
-        arrived(sums_in.at[number], r_sems, number, to_x)
-        total += sums_in[number]
+    sum_and_send(3)
+
+    total = sum_and_send(0)
+    spread_scale(1)
+    for dy in (1, 3, 2):
+        arrived(sums_in.at[dy], r_sems, 3 + dy, to_x)
+        total += sums_in[dy]
     embed[seq] = total
-    for number in range(1, 8):
+
+    def send_embedded(number):
         copy_to(embed.at[seq], embed.at[seq], g_sems, number, (seq_at(number), vocab))
-    start_scale(1, total)
-
-    def project(source, which, weight_ref, z_at):
-        normed = []
-        for i in range(2):
-            values = source[2 * z_at + i].astype(jnp.float32) * scale_slots[which, 2 * z_at + i, 0:1]
-            normed.append((values * gains[which]).astype(jnp.bfloat16))
+
+    order = (0, 2, 6, 1, 4, 3, 7, 5)
+    blocks = [seq] + [2 * lax.rem(y + 4 - n // 2, 4) + near_or_other(n % 2) for n in order[1:]]
+    for number in order[1:]:
+        send_embedded(number)
+
+    def project(source, scale, gain, weight_ref):
+        values = source.astype(jnp.float32) * scale * gain
         return lax.dot_general(
-            jnp.concatenate(normed, axis=1), weight_ref[...], (((0,), (0,)), ((), ())),
+            values.astype(jnp.bfloat16), weight_ref[...], (((0,), (0,)), ((), ())),
             preferred_element_type=jnp.float32,
-        ).reshape(2, 2, 64, 896)
+        ).reshape(2, 64, 896)
 
     arrived(hidden.at[above], h_sems, 2, to_y_up)
     arrived(hidden.at[other_below], h_sems, 3, to_y_down)
     arrived(hidden.at[far], h_sems, 5, to_y_down)
     arrived(hidden.at[other_far], h_sems, 6, to_y_up)
     end_scale(0)
-    distances = (2, 1, 3, 0)
-    for k in range(4):
-        projected[k] = project(hidden, 0, proj_hidden_ref, lax.rem(z + distances[k], 4))
-        if k == 1:
-            spread_scale(1)
-    for number in range(1, 8):
-        sender = 2 * lax.rem(y + 4 - number // 2, 4) + near_or_other(number % 2)
-        arrived(embed.at[sender], g_sems, number, to_x)
+    for k, block in enumerate(blocks):
+        projected[k] = project(hidden[block], scale_slots[0, block, 0:1], gains[0], proj_hidden_ref)
     end_scale(1)
 
+    late = []
+
     def hand_on(k):
+        block = blocks[k]
         arrived(pair_in.at[k], p_sems, k, to_pair)
-        both = projected[k, :, core] + pair_in[k]
-        z_out[k] = both.astype(jnp.bfloat16)
-        dz = distances[k]
-        for e in range(2):
-            number = 2 * dz + e
-            x_at = x_lo if e == 0 else 1 - x_lo
-            if number:
-                to = (seq, 4 * lax.rem(z + dz, 4) + 2 * x_at + core)
-                copy_to(z_out.at[k, x_at], z_in.at[number], z_sems, number, to)
-            else:
-                projected[k, :, core] = both
-
-    for k in range(4):
-        projected[k] += project(embed, 1, proj_embed_ref, lax.rem(z + distances[k], 4))
-        copy_to(projected.at[k, :, 1 - core], pair_in.at[k], p_sems, k, to_pair)
+        both = projected[k, core] + pair_in[k]
+        copy = pltpu.make_async_remote_copy(
+            src_ref=z_out.at[k], dst_ref=z_in.at[mine], send_sem=z_send.at[k], recv_sem=z_recv.at[mine],
+            device_id=(seq, 2 * block + core), device_id_type=MESH,
+        )
+        late.append((copy, block != mine))
+
+        @pl.when(block != mine)
+        def _():
+            z_out[k] = both.astype(jnp.bfloat16)
+            copy.start()
+
+        @pl.when(block == mine)
+        def _():
+            own[...] = both
+
+    for k, block in enumerate(blocks):
+        if k:
+            arrived(embed.at[block], g_sems, order[k], to_x)
+        projected[k] += project(embed[block], embed_scale[pl.ds(block, 1)], gains[1], proj_embed_ref)
+        copy_to(projected.at[k, 1 - core], pair_in.at[k], p_sems, k, to_pair)
         if k:
             hand_on(k - 1)
-    hand_on(3)
-    total = projected[3, x_lo, core]
+    hand_on(7)
+
+    total = own[...]
     for number in range(1, 8):
-        arrived(z_in.at[number], z_sems, number, to_pair)
-        total += z_in[number].astype(jnp.float32)
+        x_at = x_lo if number % 2 == 0 else 1 - x_lo
+        sender = 2 * lax.rem(z + number // 2, 4) + x_at
+        pltpu.make_async_remote_copy(
+            src_ref=z_in.at[sender], dst_ref=z_in.at[sender], send_sem=z_send.at[0], recv_sem=z_recv.at[sender],
+            device_id=to_pair, device_id_type=MESH,
+        ).wait_recv()
+        total += z_in[sender].astype(jnp.float32)
+    for copy, there in late:
+
+        @pl.when(there)
+        def _():
+            copy.wait_send()
+
     return total, sent
 
 
@@ -254,14 +291,18 @@
     pltpu.VMEM((8, 448, 128), jnp.bfloat16),
     pltpu.VMEM((2, 448, 128), jnp.float32),
     pltpu.VMEM((4, 2, 448, 128), jnp.bfloat16),
-    pltpu.VMEM((8, 448, 128), jnp.bfloat16),
+    pltpu.VMEM((4, 448, 128), jnp.bfloat16),
+    pltpu.VMEM((4, 448, 128), jnp.bfloat16),
+    pltpu.VMEM((4, 448, 128), jnp.bfloat16),
     pltpu.VMEM((2, 16, 8, 128), jnp.float32),
     pltpu.VMEM((2, 8, 8, 128), jnp.float32),
-    pltpu.VMEM((4, 2, 2, 64, 896), jnp.float32),
-    pltpu.VMEM((4, 2, 64, 896), jnp.float32),
-    pltpu.VMEM((4, 2, 64, 896), jnp.bfloat16),
+    pltpu.VMEM((8, 128), jnp.float32),
+    pltpu.VMEM((8, 2, 64, 896), jnp.float32),
+    pltpu.VMEM((8, 64, 896), jnp.float32),
     pltpu.VMEM((8, 64, 896), jnp.bfloat16),
-    *[pltpu.SemaphoreType.DMA((count,)) for count in (7, 7, 8, 8, 8, 8, 30, 30, 21, 21, 4, 4, 8, 8)],
+    pltpu.VMEM((8, 64, 896), jnp.bfloat16),
+    pltpu.VMEM((64, 896), jnp.float32),
+    *[pltpu.SemaphoreType.DMA((count,)) for count in (7, 7, 8, 8, 8, 8, 30, 30, 21, 21, 8, 8, 8, 8)],
     pltpu.SemaphoreType.DMA((1,)),
 ]
 

time: 143 us -> 141 us (0.986)
  Pallas kernels: 140 us -> 138 us
    pallas_call x1, Pallas kernels: 129 us -> 127 us  [whole(): pl.pallas_call(whole_kernel, out_shape=(pltpu.VMEM((512, 1024), jnp.bfloa...]
where the time goes in v5:
time: 141 us; the launch traced here: 140 us
  Pallas kernels  138 us (98%)
  between operations  2.33 us (2%)
    pallas_call x1, Pallas kernels, whole(): pl.pallas_call(whole_kernel, out_shape=(pltpu.VMEM((512, 1024), jnp.bfloa...  127 us
    pallas_call x1, Pallas kernels, head_gradient(): pl.pallas_call(grad_kernel, out_shape=jax.ShapeDtypeStruct((512, D), jnp....  11.1 us

profile of v5, /device:TPU:1, one launch (start us, length us, event | category | flops | bytes accessed | tf_op | source)
XLA Modules:
  0.0 140.5 jit_solution(11884169441979956126)
XLA Ops:
  0.6 127.1 %shard_map.113 = (bf16[512,1024]{1,0:T(8,128)(2,1)S(1)}, f32[1,1]{1,0:T(1,128)}, bf16[4,4,4,2,64,896]{5,4,3,2,1,0:T(8,128)(2,1)S(1)}) custom-call(bf16[448,128]{1,0:T(8,128)(2,1)} %bitcast.9, s32[1,128]{1,0:T(1,128)} %bitcast.13, s32[1,128]{1,0:T(1,128)} %bitcast.14, bf16[448,8192]{1,0:T(8,128)(2,1)} %bitcast.8, f32[1,448]{1,0:T(1,128)} %bitcast.11, ...), custom_call_target="tpu_custom_call" | custom-call | tf_op jit(solution)/shard_map/pallas_call | solution.py:584
  127.7 11.1 %shard_map.114 = bf16[512,7168]{1,0:T(8,128)(2,1)} custom-call(bf16[512,1024]{1,0:T(8,128)(2,1)S(1)} %get-tuple-element.6.grad_ref, bf16[4,4,4,2,64,896]{5,4,3,2,1,0:T(8,128)(2,1)S(1)} %get-tuple-element.7.rows_ref), custom_call_target="tpu_custom_call" | custom-call | tf_op jit(solution)/shard_map/pallas_call | solution.py:637

commit v6 on v5

--- a/solution.py
+++ b/solution.py
@@ -92,7 +92,7 @@
     embed_scale, projected, pair_in, z_out, z_in, own,
     h_send, h_recv, r_send, r_recv, g_send, g_recv, v_send, v_recv, q_send, q_recv,
     p_send, p_recv, z_send, z_recv, table_sem,
-    vocab_peers, seq_peers,
+    vocab_peers, seq_peers, start_head,
 ):
     pos, core = coordinates()
     x, y, z = pos
@@ -152,6 +152,7 @@
             gains[which, first : min(first + 128, 448)] = row_to_columns(row)[: min(448 - first, 128)]
     all_from_all(tokens, seq, seq_peers, q_sems, 0)
     table_copy.wait()
+    start_head()
 
     def look_up(y_at):
         ids = jnp.concatenate([tokens[2 * y_at, 0:1], tokens[2 * y_at + 1, 0:1]], axis=1) - seq * 8192
@@ -348,11 +349,14 @@
         )
         for i in range(8)
     ]
-    for copy in head_copies:
-        copy.start()
+
+    def start_head():
+        for copy in head_copies:
+            copy.start()
+
     vocab_peers = [(seq, lax.rem(vocab + i, 16)) for i in range(1, 16)]
     seq_peers = [(lax.rem(seq + i, 8), vocab) for i in range(1, 8)]
-    total, sent = join_kernel(*inputs, *join_scratch, vocab_peers, seq_peers)
+    total, sent = join_kernel(*inputs, *join_scratch, vocab_peers, seq_peers, start_head)
     copy_to = functools.partial(start_copy, sent)
     f_sems, stat_sems = (f_send, f_recv), (stat_send, stat_recv)
 
@@ -442,9 +446,9 @@
             if step == 0:
                 send(0, unit(part, pos, None), up(a))
                 send(1, unit(part, pos, None), down(a))
+                send(2, unit(part, pos, None), shifted(pos, a, 2))
             elif step == 1:
                 recv(0, unit(part, down(a), None))
-                send(2, unit(part, down(a), None), up(a))
                 recv(1, unit(part, up(a), None))
                 recv(2, unit(part, shifted(pos, a, 2), None))
                 send(3, unit(part, pos, a), up(b))
@@ -514,9 +518,10 @@
         10: [(2, 0, 0), (1, 1, 0), (0, 0, 1), (-1, 0, 1), (1, 0, 1)],
         11: [(2, 1, 0), (2, 0, 1), (0, 1, 1), (-1, 1, 1), (1, 1, 1), (2, 1, 1)],
     }
+    turns = (0, 1, 2, 4, 3, 5, 6, 7, 8, 9, 10, 11)
     for step in range(13):
         if step < 12:
-            by_core(own_step, step)
+            by_core(own_step, turns[step])
         if step == 0:
             start_scale()
             to_score_order(join_scratch[1][:, 1], targets)
@@ -528,7 +533,7 @@
         elif step == 5:
             end_scale()
         if step >= 2:
-            by_core(pair_step, step - 1)
+            by_core(pair_step, turns[step - 1])
             for dy, other, part in ready.get(step - 1, []):
                 multiply(dy, other, part)
 
@@ -623,24 +628,48 @@
     )(*arguments)
 
 
-def grad_kernel(grad_ref, rows_ref, out_ref):
-    y_at, hi_at = lax.div(pl.program_id(0), 2), lax.rem(pl.program_id(0), 2)
-    high = rows_ref[pl.ds(2 * hi_at, 2), y_at, :, :, 0:HIGH, :].reshape(16 * HIGH, 896)
-    low = rows_ref[pl.ds(2 * hi_at, 2), y_at, :, :, HIGH:64, :].reshape(16 * LOW, 896)
-    out_ref[...] = (
-        jnp.dot(grad_ref[:, : 16 * HIGH], high, preferred_element_type=jnp.float32)
-        + jnp.dot(grad_ref[:, 16 * HIGH :], low, preferred_element_type=jnp.float32)
-    ).astype(jnp.bfloat16)
+GRAD_COLUMNS = 1024
+
+
+def grad_kernel(grad_ref, rows_ref, out_ref, results, sems):
+    def taken(first, last):
+        pieces = []
+        while first < last:
+            block = first // 896
+            stop = min(last, 896 * block + 896)
+            rows = [
+                rows_ref[2 * (block % 2) : 2 * (block % 2) + 2, block // 2, :, :, start : start + count]
+                .reshape(16 * count, 896)[:, first - 896 * block : stop - 896 * block]
+                for start, count in ROWS
+            ]
+            pieces.append(jnp.concatenate(rows, axis=0))
+            first = stop
+        return pieces[0] if len(pieces) == 1 else jnp.concatenate(pieces, axis=1)
+
+    copies = []
+    for first in range(0, D, GRAD_COLUMNS):
+        product = jnp.dot(
+            grad_ref[...], taken(first, first + GRAD_COLUMNS), preferred_element_type=jnp.float32
+        )
+        columns = pl.ds(first, GRAD_COLUMNS)
+        results[:, columns] = product.astype(jnp.bfloat16)
+        copies.append(pltpu.make_async_copy(results.at[:, columns], out_ref.at[:, columns], sems.at[len(copies)]))
+        copies[-1].start()
+    for copy in copies:
+        copy.wait()
 
 
 def head_gradient(grad, rows):
     return pl.pallas_call(
         grad_kernel,
         out_shape=jax.ShapeDtypeStruct((512, D), jnp.bfloat16),
-        grid=(8,),
         in_specs=[pl.BlockSpec(memory_space=pltpu.VMEM)] * 2,
-        out_specs=pl.BlockSpec((512, 896), lambda i: (0, i)),
-        compiler_params=pltpu.CompilerParams(vmem_limit_bytes=24 * 1024 * 1024),
+        out_specs=pl.BlockSpec(memory_space=pl.ANY),
+        scratch_shapes=[
+            pltpu.VMEM((512, D), jnp.bfloat16),
+            pltpu.SemaphoreType.DMA((D // GRAD_COLUMNS,)),
+        ],
+        compiler_params=pltpu.CompilerParams(vmem_limit_bytes=34 * 1024 * 1024),
     )(pltpu.with_memory_space_constraint(grad, pltpu.VMEM), pltpu.with_memory_space_constraint(rows, pltpu.VMEM))
 
 

time: 141 us -> 135 us (0.957)
  Pallas kernels: 138 us -> 132 us
    pallas_call x1, Pallas kernels: 127 us -> 124 us  [whole(): pl.pallas_call(whole_kernel, out_shape=(pltpu.VMEM((512, 1024), jnp.bfloa...]
    pallas_call x1, Pallas kernels: 11.1 us -> 8.79 us  [head_gradient(): pl.pallas_call(grad_kernel, out_shape=jax.ShapeDtypeStruct((512, D), jnp....]
where the time goes in v6:
time: 135 us
  Pallas kernels  132 us (98%)
  between operations  2.33 us (2%)
    pallas_call x1, Pallas kernels, whole(): pl.pallas_call(whole_kernel, out_shape=(pltpu.VMEM((512, 1024), jnp.bfloa...  124 us
    pallas_call x1, Pallas kernels, head_gradient(): pl.pallas_call(grad_kernel, out_shape=jax.ShapeDtypeStruct((512, D), jnp....  8.79 us

profile of v6, /device:TPU:1, one launch (start us, length us, event | category | flops | bytes accessed | tf_op | source)
XLA Modules:
  0.0 134.6 jit_solution(1004629774794507261)
XLA Ops:
  0.6 123.5 %shard_map.113 = (bf16[512,1024]{1,0:T(8,128)(2,1)S(1)}, f32[1,1]{1,0:T(1,128)}, bf16[4,4,4,2,64,896]{5,4,3,2,1,0:T(8,128)(2,1)S(1)}) custom-call(bf16[448,128]{1,0:T(8,128)(2,1)} %bitcast.9, s32[1,128]{1,0:T(1,128)} %bitcast.13, s32[1,128]{1,0:T(1,128)} %bitcast.14, bf16[448,8192]{1,0:T(8,128)(2,1)} %bitcast.8, f32[1,448]{1,0:T(1,128)} %bitcast.11, ...), custom_call_target="tpu_custom_call" | custom-call | tf_op jit(solution)/shard_map/pallas_call | solution.py:589
  124.1 8.8 %shard_map.114 = bf16[512,7168]{1,0:T(8,128)(2,1)} custom-call(bf16[512,1024]{1,0:T(8,128)(2,1)S(1)} %get-tuple-element.6.grad_ref, bf16[4,4,4,2,64,896]{5,4,3,2,1,0:T(8,128)(2,1)S(1)} %get-tuple-element.7.rows_ref), custom_call_target="tpu_custom_call" | custom-call | tf_op jit(solution)/shard_map/pallas_call | solution.py:663

commit v7 on v6

--- a/solution.py
+++ b/solution.py
@@ -276,13 +276,7 @@
             device_id=to_pair, device_id_type=MESH,
         ).wait_recv()
         total += z_in[sender].astype(jnp.float32)
-    for copy, there in late:
-
-        @pl.when(there)
-        def _():
-            copy.wait_send()
-
-    return total, sent
+    return total, sent, late
 
 
 JOIN_SCRATCH = [
@@ -356,7 +350,7 @@
 
     vocab_peers = [(seq, lax.rem(vocab + i, 16)) for i in range(1, 16)]
     seq_peers = [(lax.rem(seq + i, 8), vocab) for i in range(1, 8)]
-    total, sent = join_kernel(*inputs, *join_scratch, vocab_peers, seq_peers, start_head)
+    total, sent, late = join_kernel(*inputs, *join_scratch, vocab_peers, seq_peers, start_head)
     copy_to = functools.partial(start_copy, sent)
     f_sems, stat_sems = (f_send, f_recv), (stat_send, stat_recv)
 
@@ -496,27 +490,29 @@
 
     x_hi = lax.div(x, 2)
 
-    def multiply(dy, other, part):
-        y_at = lax.rem(y + dy + 4, 4)
-        hi_at = lax.rem(x_hi + other, 2)
-        first, count = ROWS[part]
-        taken = rows[pl.ds(2 * hi_at, 2), y_at, :, :, pl.ds(first, count), :].reshape(-1, 896)
-        product = lax.dot_general(
-            head[2 * y_at + hi_at], taken, (((1,), (1,)), ((), ())), preferred_element_type=jnp.float32
-        )
+    def multiply(part, groups):
+        total = None
+        for dy, other in groups:
+            y_at, hi_at = lax.rem(y + dy + 4, 4), lax.rem(x_hi + other, 2)
+            first, count = ROWS[part]
+            taken = rows[pl.ds(2 * hi_at, 2), y_at, :, :, pl.ds(first, count), :].reshape(-1, 896)
+            product = lax.dot_general(
+                head[2 * y_at + hi_at], taken, (((1,), (1,)), ((), ())), preferred_element_type=jnp.float32
+            )
+            total = product if total is None else total + product
         columns = slice(0, 16 * HIGH) if part == 0 else slice(16 * HIGH, 1024)
-        if (dy, other) == (0, 0):
-            scores[:, columns] = product
+        if (0, 0) in groups:
+            scores[:, columns] = total
         else:
-            scores[:, columns] += product
+            scores[:, columns] += total
 
     ready = {
-        4: [(0, 0, 0)],
-        6: [(-1, 0, 0), (1, 0, 0)],
-        8: [(0, 1, 0)],
-        9: [(-1, 1, 0)],
-        10: [(2, 0, 0), (1, 1, 0), (0, 0, 1), (-1, 0, 1), (1, 0, 1)],
-        11: [(2, 1, 0), (2, 0, 1), (0, 1, 1), (-1, 1, 1), (1, 1, 1), (2, 1, 1)],
+        4: [(0, [(0, 0)])],
+        6: [(0, [(-1, 0), (1, 0)])],
+        8: [(0, [(0, 1)])],
+        9: [(0, [(-1, 1)])],
+        10: [(0, [(2, 0), (1, 1)]), (1, [(0, 0), (-1, 0), (1, 0)])],
+        11: [(0, [(2, 1)]), (1, [(2, 0), (0, 1), (-1, 1), (1, 1), (2, 1)])],
     }
     turns = (0, 1, 2, 4, 3, 5, 6, 7, 8, 9, 10, 11)
     for step in range(13):
@@ -534,8 +530,8 @@
             end_scale()
         if step >= 2:
             by_core(pair_step, turns[step - 1])
-            for dy, other, part in ready.get(step - 1, []):
-                multiply(dy, other, part)
+            for part, groups in ready.get(step - 1, []):
+                multiply(part, groups)
 
     first_entry = (seq * 16 + vocab) * 512
     entries = first_entry + lax.broadcasted_iota(jnp.int32, (512, 128), 0)
@@ -583,6 +579,11 @@
     by_core(finish, 0)
     for copy in sent:
         copy.wait_send()
+    for copy, there in late:
+
+        @pl.when(there)
+        def _():
+            copy.wait_send()
 
 
 def whole(*arguments):

time: 135 us -> 135 us (level)
  no operation moved by 1% of the time
where the time goes in v7:
time: 135 us
  Pallas kernels  132 us (98%)
  between operations  2.33 us (2%)
    pallas_call x1, Pallas kernels, whole(): pl.pallas_call(whole_kernel, out_shape=(pltpu.VMEM((512, 1024), jnp.bfloa...  124 us
    pallas_call x1, Pallas kernels, head_gradient(): pl.pallas_call(grad_kernel, out_shape=jax.ShapeDtypeStruct((512, D), jnp....  8.79 us

profile of v7, /device:TPU:1, one launch (start us, length us, event | category | flops | bytes accessed | tf_op | source)
XLA Modules:
  0.0 134.8 jit_solution(7686313482448903471)
XLA Ops:
  0.6 123.6 %shard_map.113 = (bf16[512,1024]{1,0:T(8,128)(2,1)S(1)}, f32[1,1]{1,0:T(1,128)}, bf16[4,4,4,2,64,896]{5,4,3,2,1,0:T(8,128)(2,1)S(1)}) custom-call(bf16[448,128]{1,0:T(8,128)(2,1)} %bitcast.9, s32[1,128]{1,0:T(1,128)} %bitcast.13, s32[1,128]{1,0:T(1,128)} %bitcast.14, bf16[448,8192]{1,0:T(8,128)(2,1)} %bitcast.8, f32[1,448]{1,0:T(1,128)} %bitcast.11, ...), custom_call_target="tpu_custom_call" | custom-call | tf_op jit(solution)/shard_map/pallas_call | solution.py:590
  124.3 8.8 %shard_map.114 = bf16[512,7168]{1,0:T(8,128)(2,1)} custom-call(bf16[512,1024]{1,0:T(8,128)(2,1)S(1)} %get-tuple-element.6.grad_ref, bf16[4,4,4,2,64,896]{5,4,3,2,1,0:T(8,128)(2,1)S(1)} %get-tuple-element.7.rows_ref), custom_call_target="tpu_custom_call" | custom-call | tf_op jit(solution)/shard_map/pallas_call | solution.py:664
